TPU v7x, 512 devices: a whole 4x8x8 slice. The times are simulated.
512 devices in a mesh: ctx: 32 (over y_hi, z, core), adp: 16 (over y_lo, x).
Axes of the slice: x: 4, y: 8 (y_hi: 2, y_lo: 4; y = y_hi * 4 + y_lo), z: 8, core: 2. Of those that a mesh axis runs over, the one named last changes fastest.
Arguments:
- queries: bfloat16 [8192, 4096], P('ctx', 'adp'), may hold values from -100 to 100
- keys: bfloat16 [8192, 512], P('ctx'), may hold values from -5 to 5
- values: bfloat16 [8192, 512], P('ctx'), may hold values from -6 to 6
- grad_out: bfloat16 [8192, 4096], P('ctx', 'adp'), may hold values from -6 to 6
- docs: int32 [8192], P('ctx'), may hold values from 0 to 63, never falling along the last dimension, each value on 1 to 6144 neighbouring positions
- block_tenant: int32 [64], P('ctx'), may hold values from 0 to 15
- low_rank: bfloat16 [8192, 64], P('ctx'), may hold values from -6 to 6
- adapter_b: bfloat16 [16, 64, 4096], P('adp'), may hold values from -0.75 to 0.75
Outputs:
- grad_queries: bfloat16 [8192, 4096], P('ctx', 'adp')
- grad_low_rank: float32 [8192, 64], P(('ctx', 'adp'))
- grad_adapter: float32 [16, 64, 4096], P('adp', None, 'ctx')
Inputs may be any that keep to these rules, and one draw needn't show every extreme that they name: docs never falls from one position to the next.
All inputs are finite; a program needn't handle non-finite values.
Results may differ from a plain program's by a relative error of at most 0.019.
Values may be sent and summed in bfloat16 or wider, within the bound.
A program may use at most 64 MiB of HBM per device.

v0:
```python
import jax
import jax.numpy as jnp
from jax import lax
from jax.sharding import PartitionSpec as P

QH = 32
KVH = 4
HD = 128
RANK = 64
BLOCK = 128


adapter_scale_factor = 2.0
far_below = -1e30


def key_blocks(fold_state, key_piece, update):
    key_part, value_part, doc_part = key_piece
    key_total_count = key_part.shape[0]
    block_span = 512

    def advance(step_index, current):
        offset = step_index * block_span
        return update(
            current,
            lax.dynamic_slice_in_dim(key_part, offset, block_span, 0),
            lax.dynamic_slice_in_dim(value_part, offset, block_span, 0),
            lax.dynamic_slice_in_dim(doc_part, offset, block_span, 0),
            offset,
        )

    return lax.fori_loop(0, key_total_count // block_span, advance, fold_state)


def allowed(query_pos, query_doc, doc_block, key_start):
    key_pos = key_start + jnp.arange(doc_block.shape[0], dtype=jnp.int32)
    return (key_pos[None, :] <= query_pos[:, None]) & (doc_block[None, :] == query_doc[:, None])


def on_device(queries, keys, values, grad_out, docs, block_tenant, low_rank, adapter_b):
    tokens = queries.shape[0]
    heads_dev = queries.shape[1] // HD
    kv_head = lax.axis_index("adp") * heads_dev // (QH // KVH)
    my_keys = lax.dynamic_slice_in_dim(keys, kv_head * HD, HD, 1)
    my_values = lax.dynamic_slice_in_dim(values, kv_head * HD, HD, 1)
    query_rows = (
        queries.reshape(tokens, heads_dev, HD).transpose(1, 0, 2).reshape(heads_dev * tokens, HD)
    )
    grad_rows = (
        grad_out.reshape(tokens, heads_dev, HD).transpose(1, 0, 2).reshape(heads_dev * tokens, HD)
    )
    first_pos = lax.axis_index("ctx") * tokens
    query_pos = jnp.tile(first_pos + jnp.arange(tokens, dtype=jnp.int32), heads_dev)
    query_doc = jnp.tile(docs, heads_dev)
    logit_scale = HD ** (-0.5)
    row_count = heads_dev * tokens

    def forward_update(current, key_block, value_block, doc_block, key_start):
        row_top, row_total, weighted = current
        scores = (
            jnp.einsum("qd,kd->qk", query_rows, key_block, preferred_element_type=jnp.float32)
            * logit_scale
        )
        visible = allowed(query_pos, query_doc, doc_block, key_start)
        updated_running_max = jnp.maximum(
            row_top, jnp.max(jnp.where(visible, scores, far_below), axis=1)
        )
        decay_factor = jnp.exp(row_top - updated_running_max)
        weights_f = jnp.where(visible, jnp.exp(scores - updated_running_max[:, None]), 0.0)
        row_total = row_total * decay_factor + jnp.sum(weights_f, axis=1)
        weighted = weighted * decay_factor[:, None] + jnp.dot(
            weights_f.astype(jnp.bfloat16), value_block, preferred_element_type=jnp.float32
        )
        return (updated_running_max, row_total, weighted)

    start_state = (
        jnp.full((row_count,), far_below, jnp.float32),
        jnp.zeros((row_count,), jnp.float32),
        jnp.zeros((row_count, HD), jnp.float32),
    )
    fwd_state = key_blocks(
        start_state,
        (
            lax.all_gather(my_keys, "ctx", axis=0, tiled=True),
            lax.all_gather(my_values, "ctx", axis=0, tiled=True),
            lax.all_gather(docs, "ctx", axis=0, tiled=True),
        ),
        update=forward_update,
    )
    row_top, row_total, weighted = fwd_state
    log_total = row_top + jnp.log(row_total)
    row_delta = jnp.sum(grad_rows.astype(jnp.float32) * (weighted / row_total[:, None]), axis=1)

    def backward_update(grad_acc, key_block, value_block, doc_block, key_start):
        scores = (
            jnp.einsum("qd,kd->qk", query_rows, key_block, preferred_element_type=jnp.float32)
            * logit_scale
        )
        visible = allowed(query_pos, query_doc, doc_block, key_start)
        weights_f = jnp.where(visible, jnp.exp(scores - log_total[:, None]), 0.0)
        grad_weights = jnp.einsum(
            "qd,kd->qk", grad_rows, value_block, preferred_element_type=jnp.float32
        )
        grad_scores = (weights_f * (grad_weights - row_delta[:, None])).astype(jnp.bfloat16)
        return grad_acc + jnp.dot(grad_scores, key_block, preferred_element_type=jnp.float32)

    zero_grad = jnp.zeros((row_count, HD), jnp.float32)
    grad_acc = key_blocks(
        zero_grad,
        (
            lax.all_gather(my_keys, "ctx", axis=0, tiled=True),
            lax.all_gather(my_values, "ctx", axis=0, tiled=True),
            lax.all_gather(docs, "ctx", axis=0, tiled=True),
        ),
        update=backward_update,
    )
    grad_queries = (
        (grad_acc * logit_scale)
        .astype(jnp.bfloat16)
        .reshape(heads_dev, tokens, HD)
        .transpose(1, 0, 2)
        .reshape(tokens, heads_dev * HD)
    )
    columns = lax.all_to_all(adapter_b, "adp", split_axis=2, concat_axis=0, tiled=True)
    blocks = tokens // BLOCK
    col_width = grad_queries.shape[1]
    grad_blocks = grad_queries.reshape(blocks, BLOCK, col_width)
    chosen = jnp.take(columns, block_tenant, axis=0)
    rank_contributions = (
        jnp.einsum("bkc,brc->bkr", grad_blocks, chosen, preferred_element_type=jnp.float32).reshape(
            tokens, RANK
        )
        * adapter_scale_factor
    )
    grad_low_rank = lax.psum_scatter(rank_contributions, "adp", scatter_dimension=0, tiled=True)
    low_blocks = low_rank.reshape(blocks, BLOCK, RANK)
    block_partials = jnp.einsum(
        "bkr,bkc->brc", low_blocks, grad_blocks, preferred_element_type=jnp.float32
    )
    tenants = columns.shape[0]
    tenant_membership = (
        jnp.arange(tenants, dtype=jnp.int32)[:, None] == block_tenant[None, :]
    ).astype(jnp.float32)
    tenant_contributions = (
        jnp.sum(tenant_membership[:, :, None, None] * block_partials[None], axis=1)
        * adapter_scale_factor
    )
    summed_all = lax.psum(tenant_contributions, "ctx")
    owner_view = lax.all_to_all(summed_all, "adp", split_axis=0, concat_axis=2, tiled=True)
    col_share = owner_view.shape[2] // lax.axis_size("ctx")
    grad_adapter = lax.dynamic_slice_in_dim(
        owner_view, lax.axis_index("ctx") * col_share, col_share, 2
    )
    return (grad_queries, grad_low_rank, grad_adapter)


def solution(mesh):
    placed = (
        P("ctx", "adp"),
        P("ctx", None),
        P("ctx", None),
        P("ctx", "adp"),
        P("ctx"),
        P("ctx"),
        P("ctx", None),
        P("adp", None, None),
    )
    return jax.shard_map(
        on_device,
        mesh=mesh,
        in_specs=placed,
        out_specs=(P("ctx", "adp"), P(("ctx", "adp"), None), P("adp", None, "ctx")),
        check_vma=False,
    )
```

profile of v0, /device:TPU:1, one launch (start us, length us, event | category | flops | bytes accessed | tf_op | source)
XLA Modules:
  0.0 753.9 jit_solution(9476133303147049886)
XLA Ops:
  8.8 1.5 constant_dynamic-slice_fusion.1
  10.4 61.9 %all-gather = s32[32,1,256]{2,1,0:T(1,128)S(1)} all-gather(s32[1,1,256]{2,1,0:T(1,128)} %bitcast.122), channel_id=1, replica_groups=mesh['ctx'=32,'adp'=16] {'ctx'}, dimensions={0}, use_global_device_ids=true | all-gather | bytes 33792 | tf_op jit(solution)/shard_map/all_gather | solution.py:113
  74.8 33.4 %all-gather.4.cloned.1.call-done = bf16[8192,128]{1,0:T(8,128)(2,1)} async-done(((bf16[256,128]{1,0:T(8,128)(2,1)}), bf16[8192,128]{1,0:T(8,128)(2,1)}) %all-gather.4.cloned.1.call-update) | async-done | bytes 2097168 | tf_op jit(solution)/shard_map/all_gather | solution.py:111
  108.3 90.6 %all-gather.6.cloned.1.call-done = bf16[8192,128]{1,0:T(8,128)(2,1)} async-done(((bf16[256,128]{1,0:T(8,128)(2,1)}), bf16[8192,128]{1,0:T(8,128)(2,1)}) %all-gather.6.cloned.1.call-update) | async-done | bytes 2097168 | tf_op jit(solution)/shard_map/all_gather | solution.py:112
  198.8 63.1 %while.32 = (s32[]{:T(128)}, f32[512]{0:T(512)S(1)}, f32[512]{0:T(512)S(1)}, f32[512,128]{1,0:T(8,128)S(1)}, s32[8192]{0:T(1024)S(1)}, /*index=5*/bf16[8192,128]...) while((s32[]{:T(128)}, f32[512]{0:T(512)S(1)}, ...), condition=%wide.region_3.4_spmd.clone, body=%wide.region_0.3_spmd.clone.sunk | while | flops 139136000 | bytes 4141263 | solution.py:32
  199.6 1.3 select_reduce_fusion.2
  201.2 1.5 convolution_add_fusion.2
  203.5 1.3 select_reduce_fusion.2
  205.2 1.5 convolution_add_fusion.2
  207.5 1.3 select_reduce_fusion.2
  209.1 1.5 convolution_add_fusion.2
  211.4 1.3 select_reduce_fusion.2
  213.1 1.5 convolution_add_fusion.2
  215.4 1.3 select_reduce_fusion.2
  217.0 1.5 convolution_add_fusion.2
  219.3 1.3 select_reduce_fusion.2
  220.9 1.5 convolution_add_fusion.2
  223.2 1.3 select_reduce_fusion.2
  224.9 1.5 convolution_add_fusion.2
  227.2 1.3 select_reduce_fusion.2
  228.8 1.5 convolution_add_fusion.2
  231.1 1.3 select_reduce_fusion.2
  232.8 1.5 convolution_add_fusion.2
  235.1 1.3 select_reduce_fusion.2
  236.7 1.5 convolution_add_fusion.2
  239.0 1.3 select_reduce_fusion.2
  240.7 1.5 convolution_add_fusion.2
  243.0 1.3 select_reduce_fusion.2
  244.6 1.5 convolution_add_fusion.2
  246.9 1.3 select_reduce_fusion.2
  248.5 1.5 convolution_add_fusion.2
  250.8 1.3 select_reduce_fusion.2
  252.5 1.5 convolution_add_fusion.2
  254.8 1.3 select_reduce_fusion.2
  256.4 1.5 convolution_add_fusion.2
  258.7 1.3 select_reduce_fusion.2
  260.4 1.5 convolution_add_fusion.2
  262.1 60.8 %while.33 = (s32[]{:T(128)}, f32[512,128]{1,0:T(8,128)S(1)}, s32[8192]{0:T(1024)S(1)}, bf16[8192,128]{1,0:T(8,128)(2,1)}, bf16[512,128]{1,0:T(8,128)(2,1)S(1)}, ...) while((s32[]{:T(128)}, f32[512,128]{1,0:T(8,128)S(1)}, ...), condition=%wide.region_6.7_spmd.clone, body=%wide.region_5.6_spmd.clone.sunk | while | flops 203817472 | bytes 3311312 | solution.py:32
  262.2 1.2 fusion.88
  264.2 1.8 fusion.89
  267.9 1.8 fusion.89
  271.7 1.8 fusion.89
  275.5 1.8 fusion.89
  279.3 1.8 fusion.89
  283.1 1.8 fusion.89
  286.9 1.8 fusion.89
  290.7 1.8 fusion.89
  294.5 1.8 fusion.89
  298.3 1.8 fusion.89
  302.1 1.8 fusion.89
  305.9 1.8 fusion.89
  309.7 1.8 fusion.89
  313.5 1.8 fusion.89
  317.3 1.8 fusion.89
  321.1 1.8 fusion.89
  324.8 2.8 copy.50
  328.1 22.4 %reduce = bf16[4096,64]{1,0:T(8,128)(2,1)S(1)} reduce(bf16[4096,1,64]{2,1,0:T(2,128)(2,1)S(1)} %bitcast.105, bf16[]{:T(256)} %broadcast.112), dimensions={1}, to_apply=%bitcast.66.reduce_sub_computation | reduce | bytes 1048578
  351.2 22.2 %all_to_all.36 = bf16[16,2,8192]{2,1,0:T(2,128)(2,1)S(1)} all-to-all(bf16[16,2,8192]{2,1,0:T(2,128)(2,1)S(1)} %reshape.100), channel_id=1, replica_groups=mesh['ctx'=32,'adp'=16] {'adp'}, dimensions={0} | all-to-all | bytes 1048576 | tf_op jit(solution)/shard_map/all_to_all | solution.py:124
  373.4 292.6 %all-reduce.2.cloned.1.call-done = f32[16,64,256]{2,1,0:T(8,128)} async-done(((f32[16,64,256]{2,1,0:T(8,128)}), f32[16,64,256]{2,1,0:T(8,128)}) %all-reduce.2.cloned.1.call-update) | async-done | bytes 1048592 | tf_op jit(solution)/shard_map/psum | solution.py:148
  666.0 4.5 all-to-all-start.1
  670.6 1.2 reshape.101
  675.5 17.2 %all-to-all-done.1 = f32[16,64,256]{2,1,0:T(8,128)} async-done(((f32[16,64,256]{2,1,0:T(8,128)}), f32[16,64,256]{2,1,0:T(8,128)}, u32[]{:S(2)}, u32[]{:S(2)}) %all-to-all-start.1) | async-done | bytes 1048608 | tf_op jit(solution)/shard_map/all_to_all | solution.py:149
  692.7 1.3 copy.71
  694.6 52.7 %reduce-scatter.4.cloned.1.call-done = f32[16,64]{1,0:T(8,128)} async-done(((f32[256,64]{1,0:T(8,128)}), f32[16,64]{1,0:T(8,128)}) %reduce-scatter.4.cloned.1.call-update) | async-done | bytes 4112
  (286 shorter events, 59.9 us)
Async XLA Ops:
  7.2 1.0 copy-start
  7.2 101.1 %all-gather.4.cloned.1.call-start = ((), (), s32[]{:S(2)}) async-start(), calls=%async_computation.3 | async-start | bytes 2162688 | tf_op jit(solution)/shard_map/all_gather | solution.py:111
  8.8 190.0 %all-gather.6.cloned.1.call-start = ((), (), s32[]{:S(2)}) async-start(), calls=%async_computation.4 | async-start | bytes 2162688 | tf_op jit(solution)/shard_map/all_gather | solution.py:112
  10.3 655.7 %all-reduce.2.cloned.1.call-start = ((), (), s32[]{:S(2)}) async-start(), calls=%async_computation.5 | async-start | bytes 2097152 | tf_op jit(solution)/shard_map/psum | solution.py:148
  262.1 61.1 %copy-start.3 = (bf16[256,64]{0,1:T(8,128)(2,1)S(1)}, bf16[256,64]{0,1:T(8,128)(2,1)}, u32[]{:S(2)}) copy-start(bf16[256,64]{0,1:T(8,128)(2,1)} %param.18) | copy-start | bytes 98308
  323.2 1.5 copy-start.1
  323.4 1.4 copy-start.2
  350.5 320.0 %copy-start.4 = (s32[2]{0:T(128)S(1)}, s32[2]{0:T(128)}, u32[]{:S(2)}) copy-start(s32[2]{0:T(128)} %param.17) | copy-start | bytes 28
  666.0 26.7 %all-to-all-start.1 = ((f32[16,64,256]{2,1,0:T(8,128)}), f32[16,64,256]{2,1,0:T(8,128)}, u32[]{:S(2)}, u32[]{:S(2)}) async-start(f32[16,64,256]{2,1,0:T(8,128)} %all-reduce.2.cloned.1.call-done), calls=%async_computation.1 | async-start | bytes 2097152 | tf_op jit(solution)/shard_map/all_to_all | solution.py:149
  670.5 76.8 %reduce-scatter.4.cloned.1.call-start = ((), (), s32[]{:S(2)}) async-start(), calls=%async_computation.6 | async-start | bytes 139264
Sparse Core Ops, SparseCore 0:
  11.9 96.2 all-gather.3
  111.6 87.1 all-gather.5
  324.9 341.0 all-reduce.1
  674.9 72.3 reduce-scatter.3
where the time goes:
time: 767 us; the launch traced here: 754 us
  waiting for transfers between devices  487 us (63%)
  matrix products  93.5 us (12%)
  blocking collectives  84.1 us (11%)
  local copies, waits for them, and re-layouts  39.3 us (5%)
  other arithmetic  30.3 us (4%)
  between operations  14 us (2%)
    psum x1, waiting for transfers between devices, on_device(): summed_all = lax.psum(tenant_contributions, 'ctx')  293 us
    all_gather x1, waiting for transfers between devices, on_device(): lax.all_gather(my_values, 'ctx', axis=0, tiled=True)  90.6 us
    all_gather x1, blocking collectives, on_device(): lax.all_gather(docs, 'ctx', axis=0, tiled=True)  61.9 us
    unnamed x5, waiting for transfers between devices  52.8 us
    all_gather x1, waiting for transfers between devices, on_device(): lax.all_gather(my_keys, 'ctx', axis=0, tiled=True)  33.4 us
    dot_general x16, matrix products, backward_update(): jnp.dot(grad_scores, key_block, preferred_element_type=jnp.float32)  28.6 us
    dot_general x16, matrix products, forward_update(): jnp.dot(weights_f.astype(jnp.bfloat16), value_block, preferred_element_ty...  23.8 us
    unnamed x5, other arithmetic  22.4 us
  transfers between devices with their start and end apart: 5, of which 5 were waited for; matrix products, arithmetic and copies ran while one was open for 5% of the time, Pallas kernels for 0%

commit v1 on v0

v1 whole, which is shorter than its diff:
```python
import math

import jax
import jax.numpy as jnp
from jax import lax
from jax.experimental import pallas as pl
from jax.experimental.pallas import tpu as pltpu
from jax.sharding import PartitionSpec as P

HD = 128
RANK = 64
TOK = 256
NZ = 8
NX = 4
NYL = 4
N_CTX = 32
N_ADP = 16
SLOT = 2 * TOK + 16
EXP2_SCALE = HD ** (-0.5) * math.log2(math.e)
FAR = -1e30
MESH = pl.DeviceIdType.MESH
F32 = jnp.float32
BF16 = jnp.bfloat16


def nt_dot(a, b):
    return lax.dot_general(a, b, (((1,), (1,)), ((), ())), preferred_element_type=F32)


def body(
    q_ref, k_ref, v_ref, go_ref, docs_ref, bt_ref, low_ref, b_ref,
    gq_ref, glr_ref, ga_ref,
    kv, xkv, acc, row_top, qdoc, bcols, btile, lowt,
    pbuf, qbuf, tbuf, gbuf, rsend, rbuf,
    loc_sem, kv_recv, plus_send, minus_send, sib_send, y_send,
    bt_recv, bt_send, b_recv, b_send, bs_recv, bs_send,
    r_recv, r_send, p_recv, p_send, g_recv, g_send,
):
    c = lax.axis_index("ctx")
    a = lax.axis_index("adp")
    core = c % 2
    pair = c // 2
    z = pair % NZ
    y_hi = pair // NZ
    head = a // NX
    x = a % NX
    sib = pair * 2 + (1 - core)
    z_plus = (y_hi * NZ + (z + 1) % NZ) * 2 + core
    z_minus = (y_hi * NZ + (z + NZ - 1) % NZ) * 2 + core
    y_ctx = ((1 - y_hi) * NZ + z) * 2 + core
    y_adp = (NYL - 1 - head) * NX + x
    selfdest = (pair == a).astype(jnp.int32)

    barrier = pltpu.get_barrier_semaphore()

    def greet(ctx, adp):
        pl.semaphore_signal(barrier, inc=1, device_id={"ctx": ctx, "adp": adp}, device_id_type=MESH)

    greet(y_ctx, y_adp)

    @pl.loop(1, N_CTX)
    def _(i):
        greet((c + i) % N_CTX, a)

    @pl.loop(1, N_ADP)
    def _(i):
        greet(c, (a + i) % N_ADP)

    @pl.loop(0, N_ADP)
    def _(i):
        @pl.when(jnp.logical_not((pair == a) & (i == pair)))
        def _():
            greet(i * 2 + core, pair)

    def col(which):
        return pl.ds(pl.multiple_of(which * HD, HD), HD)

    own_k = pltpu.make_async_copy(k_ref.at[:, col(head)], kv.at[c, pl.ds(0, TOK)], loc_sem.at[0])
    own_v = pltpu.make_async_copy(v_ref.at[:, col(head)], kv.at[c, pl.ds(TOK, TOK)], loc_sem.at[1])
    other = NYL - 1 - head
    x_k = pltpu.make_async_copy(k_ref.at[:, col(other)], xkv.at[pl.ds(0, TOK)], loc_sem.at[2])
    x_v = pltpu.make_async_copy(v_ref.at[:, col(other)], xkv.at[pl.ds(TOK, TOK)], loc_sem.at[3])
    half = pl.multiple_of(core * (RANK // 2), RANK // 2)
    own_b = pltpu.make_async_copy(
        b_ref.at[0, pl.ds(half, RANK // 2), pl.ds(pl.multiple_of(a * 2 * HD, 2 * HD), 2 * HD)],
        bcols.at[a, pl.ds(half, RANK // 2)],
        loc_sem.at[4],
    )
    own_k.start()
    own_v.start()
    x_k.start()
    x_v.start()
    own_b.start()

    doc_rows = docs_ref[...].astype(F32)
    tag = jnp.concatenate([doc_rows, jnp.zeros((14, HD), F32)], axis=0).astype(BF16)
    kv[c, pl.ds(2 * TOK, 16), :] = tag
    xkv[pl.ds(2 * TOK, 16), :] = tag
    sub8 = lax.broadcasted_iota(jnp.int32, (8, HD), 0)
    btile[c] = jnp.where(sub8 < 4, bt_ref[0], bt_ref[1])

    own_k.wait()
    own_v.wait()
    x_k.wait()
    x_v.wait()
    own_b.wait()
    pl.semaphore_wait(barrier, 1 + (N_CTX - 1) + (N_ADP - 1) + N_ADP - selfdest)

    def move(chunk, send_sem, to):
        return pltpu.make_async_remote_copy(
            src_ref=kv.at[chunk], dst_ref=kv.at[chunk],
            send_sem=send_sem.at[chunk], recv_sem=kv_recv.at[chunk],
            device_id={"ctx": to, "adp": a}, device_id_type=MESH,
        )

    def to_y():
        return pltpu.make_async_remote_copy(
            src_ref=xkv, dst_ref=kv.at[c], send_sem=y_send, recv_sem=kv_recv.at[c],
            device_id={"ctx": y_ctx, "adp": y_adp}, device_id_type=MESH,
        )

    move(c, plus_send, z_plus).start()
    move(c, minus_send, z_minus).start()
    move(c, sib_send, sib).start()

    @pl.when(y_hi == 0)
    def _():
        to_y().start()

    def bt_copy(i):
        to = (c + i) % N_CTX
        return pltpu.make_async_remote_copy(
            src_ref=btile.at[c], dst_ref=btile.at[c], send_sem=bt_send.at[to], recv_sem=bt_recv.at[c],
            device_id={"ctx": to, "adp": a}, device_id_type=MESH,
        )

    def bt_arrival(i):
        frm = (c + i) % N_CTX
        return pltpu.make_async_copy(btile.at[frm], btile.at[frm], bt_recv.at[frm])

    def b_copy(i):
        to = (a + i) % N_ADP
        return pltpu.make_async_remote_copy(
            src_ref=b_ref.at[0, pl.ds(half, RANK // 2), pl.ds(pl.multiple_of(to * 2 * HD, 2 * HD), 2 * HD)],
            dst_ref=bcols.at[a, pl.ds(half, RANK // 2)],
            send_sem=b_send.at[to], recv_sem=b_recv.at[a],
            device_id={"ctx": c, "adp": to}, device_id_type=MESH,
        )

    def b_arrival(i):
        frm = (a + i) % N_ADP
        ref = bcols.at[frm, pl.ds(half, RANK // 2)]
        return pltpu.make_async_copy(ref, ref, b_recv.at[frm])

    def b_share():
        ref = bcols.at[:, pl.ds(half, RANK // 2)]
        return pltpu.make_async_remote_copy(
            src_ref=ref, dst_ref=ref, send_sem=bs_send, recv_sem=bs_recv,
            device_id={"ctx": sib, "adp": a}, device_id_type=MESH,
        )

    def b_shared():
        ref = bcols.at[:, pl.ds(pl.multiple_of((1 - core) * (RANK // 2), RANK // 2), RANK // 2)]
        return pltpu.make_async_copy(ref, ref, bs_recv)

    @pl.loop(1, N_CTX)
    def _(i):
        bt_copy(i).start()

    @pl.loop(1, N_ADP)
    def _(i):
        b_copy(i).start()

    rr = lax.broadcasted_iota(jnp.int32, (2 * RANK, RANK), 0)
    kk = lax.broadcasted_iota(jnp.int32, (2 * RANK, RANK), 1)
    pick = jnp.where(kk == ((rr >> 3) * 4 + (rr & 3)), 1.0, 0.0).astype(BF16)
    spread = nt_dot(pick, low_ref[...])
    rr = lax.broadcasted_iota(jnp.int32, (2 * RANK, TOK), 0)
    tt = lax.broadcasted_iota(jnp.int32, (2 * RANK, TOK), 1)
    lowt[...] = jnp.where((tt >> 7) == ((rr >> 2) & 1), spread, 0.0).astype(BF16)

    ri = lax.broadcasted_iota(jnp.int32, (HD, HD), 0)
    ci = lax.broadcasted_iota(jnp.int32, (HD, HD), 1)
    for part in range(2):
        spot = jnp.where(ri == ci, jnp.broadcast_to(doc_rows[part : part + 1, :], (HD, HD)), 0.0)
        column = jnp.sum(spot, axis=1, keepdims=True)
        qdoc[pl.ds(part * HD, HD), :] = jnp.broadcast_to(column, (HD, HD))

    ones = jnp.ones((TOK, HD), BF16)

    def attend(which, first):
        low_slot = which * 2
        row_doc = qdoc[...]
        for h in range(2):
            q_h = q_ref[:, h * HD : (h + 1) * HD]
            g_h = go_ref[:, h * HD : (h + 1) * HD]
            tiles = []
            for half_pair in range(2):
                scores = nt_dot(q_h, kv[low_slot + half_pair, pl.ds(0, TOK), :])
                key_doc = kv[low_slot + half_pair, pl.ds(2 * TOK, 16), :].astype(F32)
                for lt in range(2):
                    seen = row_doc == key_doc[lt : lt + 1, :]
                    if first:
                        rpos = lax.broadcasted_iota(jnp.int32, (TOK, HD), 0) + core * TOK
                        kpos = lax.broadcasted_iota(jnp.int32, (TOK, HD), 1) + (half_pair * TOK + lt * HD)
                        seen = seen & (kpos <= rpos)
                    tiles.append(jnp.where(seen, scores[:, lt * HD : (lt + 1) * HD], FAR))
            top = jnp.maximum(jnp.maximum(tiles[0], tiles[1]), jnp.maximum(tiles[2], tiles[3]))
            top = jnp.broadcast_to(jnp.max(top, axis=1, keepdims=True), (TOK, HD))
            if not first:
                before = row_top[h]
                top = jnp.maximum(top, before)
                decay = jnp.exp2((before - top) * EXP2_SCALE)
            row_top[h] = top
            total = None
            for half_pair in range(2):
                weights = [
                    jnp.exp2((tiles[half_pair * 2 + lt] - top) * EXP2_SCALE) for lt in range(2)
                ]
                weights = jnp.concatenate(weights, axis=1)
                gw = nt_dot(g_h, kv[low_slot + half_pair, pl.ds(TOK, TOK), :])
                both = jnp.concatenate([weights.astype(BF16), (weights * gw).astype(BF16)], axis=0)
                right = jnp.concatenate([kv[low_slot + half_pair, pl.ds(0, TOK), :], ones], axis=1)
                term = jnp.dot(both, right, preferred_element_type=F32)
                total = term if total is None else total + term
            if first:
                acc[h] = total
            else:
                wide = jnp.concatenate([decay, decay], axis=1)
                wide = jnp.concatenate([wide, wide], axis=0)
                acc[h] = acc[h] * wide + total

    def arrived(chunk):
        pltpu.make_async_copy(kv.at[chunk], kv.at[chunk], kv_recv.at[chunk]).wait()

    arrived(sib)
    attend(pair, True)

    def event(e):
        s, u = e // 4, e % 4
        lower, back = u // 2, u % 2
        dist = s - lower
        valid = (dist >= 0) & (lower <= y_hi)
        valid = valid & ((dist > 0) | ((lower == 1) & (back == 0)))
        valid = valid & ((dist <= 3) | ((dist == 4) & (back != lower)))
        from_z = (z + NZ - dist + 2 * dist * back) % NZ
        src_pair = jnp.where(lower == 1, 0, y_hi) * NZ + from_z
        on_plus = valid & ((back == 0) | (dist == 0)) & ((dist <= 2) | ((dist == 3) & (lower == 1)))
        on_minus = valid & ((back == 1) | (dist == 0)) & ((dist <= 2) | ((dist == 3) & (lower == 0)))
        return valid, src_pair, on_plus, on_minus

    @pl.loop(4, 24)
    def _(e):
        valid, src_pair, on_plus, on_minus = event(e)
        chunk = src_pair * 2 + core

        @pl.when(valid)
        def _():
            arrived(chunk)

            @pl.when(on_plus)
            def _():
                move(chunk, plus_send, z_plus).start()

            @pl.when(on_minus)
            def _():
                move(chunk, minus_send, z_minus).start()

            move(chunk, sib_send, sib).start()
            arrived(src_pair * 2 + 1 - core)

            @pl.when(src_pair < pair)
            def _():
                attend(src_pair, False)

    @pl.loop(1, N_ADP)
    def _(i):
        b_arrival(i).wait()

    b_share().start()

    for h in range(2):
        total = acc[h, pl.ds(0, TOK), pl.ds(HD, HD)]
        inv = 1.0 / total
        delta = acc[h, pl.ds(TOK, TOK), pl.ds(HD, HD)] * inv
        grad = (acc[h, pl.ds(TOK, TOK), pl.ds(0, HD)] - delta * acc[h, pl.ds(0, TOK), pl.ds(0, HD)]) * inv
        gq_ref[:, h * HD : (h + 1) * HD] = (grad * HD ** (-0.5)).astype(BF16)

    gq = gq_ref[...]
    partial = jnp.dot(lowt[...], gq, preferred_element_type=F32) * 2.0
    for h in range(2):
        pbuf[h] = partial[:, h * HD : (h + 1) * HD].reshape(N_ADP, 8, HD)

    def p_copy(i):
        to = (c + i) % N_CTX
        return pltpu.make_async_remote_copy(
            src_ref=pbuf.at[to % 2, to // 2], dst_ref=qbuf.at[c],
            send_sem=p_send.at[to], recv_sem=p_recv.at[c],
            device_id={"ctx": to, "adp": a}, device_id_type=MESH,
        )

    def p_arrival(i):
        frm = (c + i) % N_CTX
        return pltpu.make_async_copy(qbuf.at[frm], qbuf.at[frm], p_recv.at[frm])

    @pl.loop(1, N_CTX)
    def _(i):
        p_copy(i).start()

    qbuf[c] = pbuf[core, pair]

    b_shared().wait()
    b_share().wait_send()
    for blk in range(2):
        chosen = bcols[bt_ref[blk]]
        padded = jnp.concatenate([chosen, jnp.zeros_like(chosen)], axis=0)
        part = nt_dot(gq[blk * HD : (blk + 1) * HD, :], padded) * 2.0
        rsend[pl.ds(blk * 8, 8)] = part.reshape(8, 16, HD)

    def r_copy(i):
        to = (a + i) % N_ADP
        return pltpu.make_async_remote_copy(
            src_ref=rsend.at[to], dst_ref=rbuf.at[a], send_sem=r_send.at[to], recv_sem=r_recv.at[a],
            device_id={"ctx": c, "adp": to}, device_id_type=MESH,
        )

    def r_arrival(i):
        frm = (a + i) % N_ADP
        return pltpu.make_async_copy(rbuf.at[frm], rbuf.at[frm], r_recv.at[frm])

    @pl.loop(1, N_ADP)
    def _(i):
        r_copy(i).start()

    rbuf[a] = rsend[a]

    @pl.loop(1, N_CTX)
    def _(i):
        bt_arrival(i).wait()
        p_arrival(i).wait()

    def add_source(i, sums):
        tile, owner = qbuf[i], btile[i]
        return tuple(s + jnp.where(owner == t, tile, 0.0) for t, s in enumerate(sums))

    sums = lax.fori_loop(0, N_CTX, add_source, tuple(jnp.zeros((8, HD), F32) for _ in range(N_ADP)))
    for t in range(N_ADP):
        tbuf[t] = sums[t]

    def g_copy(t):
        return pltpu.make_async_remote_copy(
            src_ref=tbuf.at[t], dst_ref=gbuf.at[pair], send_sem=g_send.at[t], recv_sem=g_recv.at[pair],
            device_id={"ctx": a * 2 + core, "adp": t}, device_id_type=MESH,
        )

    def g_arrival(i):
        return pltpu.make_async_copy(gbuf.at[i], gbuf.at[i], g_recv.at[i])

    def not_self(i):
        return jnp.logical_not((pair == a) & (i == a))

    @pl.loop(0, N_ADP)
    def _(i):
        t = (a + i) % N_ADP

        @pl.when(not_self(t))
        def _():
            g_copy(t).start()

    @pl.when(pair == a)
    def _():
        gbuf[pair] = tbuf[a]

    @pl.loop(1, N_ADP)
    def _(i):
        r_arrival(i).wait()

    share = rbuf[0]
    for i in range(1, N_ADP):
        share = share + rbuf[i]
    glr_ref[...] = share[:, :RANK]

    @pl.loop(0, N_ADP)
    def _(i):
        @pl.when(not_self(i))
        def _():
            g_arrival(i).wait()

    for i in range(N_ADP):
        tile = gbuf[i]
        ga_ref[0, pl.ds(i * 4, 4), :] = tile[0:4] + tile[4:8]

    move(c, plus_send, z_plus).wait_send()
    move(c, minus_send, z_minus).wait_send()
    move(c, sib_send, sib).wait_send()

    @pl.when(y_hi == 0)
    def _():
        to_y().wait_send()

    @pl.loop(4, 24)
    def _(e):
        valid, src_pair, on_plus, on_minus = event(e)
        chunk = src_pair * 2 + core

        @pl.when(on_plus)
        def _():
            move(chunk, plus_send, z_plus).wait_send()

        @pl.when(on_minus)
        def _():
            move(chunk, minus_send, z_minus).wait_send()

        @pl.when(valid)
        def _():
            move(chunk, sib_send, sib).wait_send()

    @pl.loop(1, N_CTX)
    def _(i):
        bt_copy(i).wait_send()
        p_copy(i).wait_send()

    @pl.loop(1, N_ADP)
    def _(i):
        b_copy(i).wait_send()
        r_copy(i).wait_send()

    @pl.loop(0, N_ADP)
    def _(i):
        @pl.when(not_self(i))
        def _():
            g_copy(i).wait_send()


def on_device(queries, keys, values, grad_out, docs, block_tenant, low_rank, adapter_b):
    vmem = pl.BlockSpec(memory_space=pltpu.VMEM)
    anywhere = pl.BlockSpec(memory_space=pl.ANY)
    dma = pltpu.SemaphoreType.DMA
    return pl.pallas_call(
        body,
        out_shape=(
            jax.ShapeDtypeStruct((TOK, 2 * HD), BF16),
            jax.ShapeDtypeStruct((16, RANK), F32),
            jax.ShapeDtypeStruct((1, RANK, HD), F32),
        ),
        in_specs=[
            vmem, anywhere, anywhere, vmem, vmem,
            pl.BlockSpec(memory_space=pltpu.SMEM), vmem, anywhere,
        ],
        out_specs=(vmem, vmem, vmem),
        scratch_shapes=[
            pltpu.VMEM((N_CTX, SLOT, HD), BF16),
            pltpu.VMEM((SLOT, HD), BF16),
            pltpu.VMEM((2, 2 * TOK, 2 * HD), F32),
            pltpu.VMEM((2, TOK, HD), F32),
            pltpu.VMEM((TOK, HD), F32),
            pltpu.VMEM((N_ADP, RANK, 2 * HD), BF16),
            pltpu.VMEM((N_CTX, 8, HD), jnp.int32),
            pltpu.VMEM((2 * RANK, TOK), BF16),
            pltpu.VMEM((2, N_ADP, 8, HD), F32),
            pltpu.VMEM((N_CTX, 8, HD), F32),
            pltpu.VMEM((N_ADP, 8, HD), F32),
            pltpu.VMEM((N_ADP, 8, HD), F32),
            pltpu.VMEM((N_ADP, 16, HD), F32),
            pltpu.VMEM((N_ADP, 16, HD), F32),
            dma((5,)), dma((N_CTX,)), dma((N_CTX,)), dma((N_CTX,)), dma((N_CTX,)), dma,
            dma((N_CTX,)), dma((N_CTX,)), dma((N_ADP,)), dma((N_ADP,)), dma, dma,
            dma((N_ADP,)), dma((N_ADP,)), dma((N_CTX,)), dma((N_CTX,)), dma((N_ADP,)), dma((N_ADP,)),
        ],
        compiler_params=pltpu.CompilerParams(
            collective_id=0, has_side_effects=True, vmem_limit_bytes=48 * 1024 * 1024
        ),
        cost_estimate=pl.CostEstimate(flops=4_000_000_000, bytes_accessed=4_000_000, transcendentals=4_000_000),
    )(
        queries, keys, values, grad_out, docs.reshape(2, HD), block_tenant, low_rank, adapter_b
    )


def solution(mesh):
    placed = (
        P("ctx", "adp"),
        P("ctx", None),
        P("ctx", None),
        P("ctx", "adp"),
        P("ctx"),
        P("ctx"),
        P("ctx", None),
        P("adp", None, None),
    )
    return jax.shard_map(
        on_device,
        mesh=mesh,
        in_specs=placed,
        out_specs=(P("ctx", "adp"), P(("ctx", "adp"), None), P("adp", None, "ctx")),
        check_vma=False,
    )
```

time: 767 us -> 84 us (0.11); the launches traced: 754 us -> 82.6 us
  waiting for transfers between devices: 487 us -> 0 us
  matrix products: 93.5 us -> 0 us
  blocking collectives: 84.1 us -> 0 us
  Pallas kernels: 0 us -> 74.4 us
  local copies, waits for them, and re-layouts: 39.3 us -> 7.5 us
  other arithmetic: 30.3 us -> 0 us
  between operations: 14 us -> 0.69 us
    psum x1 -> x0, waiting for transfers between devices: 293 us -> none  [on_device(): summed_all = lax.psum(tenant_contributions, 'ctx')]
    all_gather x2 -> x0, waiting for transfers between devices: 124 us -> none  [the longest x1 90.6 us: on_device(): lax.all_gather(my_values, 'ctx', axis=0, tiled=True)]
    dot_general x66 -> x0, matrix products: 93.5 us -> none  [the longest x16 28.6 us: backward_update(): jnp.dot(grad_scores, key_block, preferred_element_type=jnp.float32)]
    pallas_call x0 -> x1, Pallas kernels: none -> 74.4 us  [on_device(): pl.pallas_call(body, out_shape=(jax.ShapeDtypeStruct((TOK, 2 * HD), BF16)...]
    all_gather x1 -> x0, blocking collectives: 61.9 us -> none  [on_device(): lax.all_gather(docs, 'ctx', axis=0, tiled=True)]
    unnamed x5 -> x0, waiting for transfers between devices: 52.8 us -> none
    unnamed x5 -> x0, other arithmetic: 22.4 us -> none
    all_to_all x1 -> x0, blocking collectives: 22.2 us -> none  [on_device(): lax.all_to_all(adapter_b, 'adp', split_axis=2, concat_axis=0, tiled=True)]
  transfers between devices with their start and end apart: 5 -> 0, of which waited for: 5 -> 0; matrix products, arithmetic and copies ran while one was open for 5% -> 0% of each run, Pallas kernels for 0% -> 0%
where the time goes in v1:
time: 84 us; the launch traced here: 82.6 us
  Pallas kernels  74.4 us (89%)
  local copies, waits for them, and re-layouts  7.5 us (9%)
    pallas_call x1, Pallas kernels, on_device(): pl.pallas_call(body, out_shape=(jax.ShapeDtypeStruct((TOK, 2 * HD), BF16)...  74.4 us
    unnamed x18, local copies, waits for them, and re-layouts  7.5 us

profile of v1, /device:TPU:1, one launch (start us, length us, event | category | flops | bytes accessed | tf_op | source)
XLA Modules:
  0.0 82.6 jit_solution(13453745558961528451)
XLA Ops:
  0.6 0.0 copy-start.5
  0.6 0.0 copy-start.6
  0.7 0.9 %copy.11.low_ref = bf16[256,64]{1,0:T(8,128)(2,1)S(1)} copy(bf16[256,64]{0,1:T(8,128)(2,1)} %param.14) | data formatting | bytes 65536 | tf_op args[6]
  1.5 0.0 copy-done.5
  1.5 0.0 copy-done.6
  1.6 0.0 copy-start
  1.6 1.0 %copy-done = bf16[1,64,4096]{2,1,0:T(8,128)(2,1)S(1)} copy-done((bf16[1,64,4096]{2,1,0:T(8,128)(2,1)S(1)}, bf16[1,64,4096]{2,1,0:T(8,128)(2,1)}, u32[]{:S(2)}) %copy-start) | copy-done | bytes 524312
  2.6 0.0 copy-start.1
  2.6 0.9 %copy-done.1 = bf16[256,512]{1,0:T(8,128)(2,1)S(1)} copy-done((bf16[256,512]{1,0:T(8,128)(2,1)S(1)}, bf16[256,512]{1,0:T(8,128)(2,1)}, u32[]{:S(2)}) %copy-start.1) | copy-done | bytes 262168
  3.6 0.0 copy-start.2
  3.6 0.9 %copy-done.2 = bf16[256,512]{1,0:T(8,128)(2,1)S(1)} copy-done((bf16[256,512]{1,0:T(8,128)(2,1)S(1)}, bf16[256,512]{1,0:T(8,128)(2,1)}, u32[]{:S(2)}) %copy-start.2) | copy-done | bytes 262168
  4.5 0.0 copy-start.3
  4.5 0.9 %copy-done.3 = bf16[256,256]{1,0:T(8,128)(2,1)S(1)} copy-done((bf16[256,256]{1,0:T(8,128)(2,1)S(1)}, bf16[256,256]{1,0:T(8,128)(2,1)}, u32[]{:S(2)}) %copy-start.3) | copy-done | bytes 131096
  5.4 0.0 copy-start.4
  5.4 0.9 %copy-done.4 = bf16[256,256]{1,0:T(8,128)(2,1)S(1)} copy-done((bf16[256,256]{1,0:T(8,128)(2,1)S(1)}, bf16[256,256]{1,0:T(8,128)(2,1)}, u32[]{:S(2)}) %copy-start.4) | copy-done | bytes 131096
  6.3 74.4 %shard_map.103 = (bf16[256,256]{1,0:T(8,128)(2,1)S(1)}, f32[16,64]{1,0:T(8,128)S(1)}, f32[1,64,128]{2,1,0:T(8,128)S(1)}) custom-call(bf16[256,256]{1,0:T(8,128)(2,1)S(1)} %copy-done.3, bf16[256,512]{1,0:T(8,128)(2,1)S(1)} %copy-done.1, bf16[256,512]{1,0:T(8,128)(2,1)S(1)} %copy-done.2, bf16[256,256]{1,0:T(8,128)(2,1)S(1)} %copy-done.4, ...), custom_call_target="tpu_custom_call" | custom-call | flops 4000000000 | bytes 4000000 | tf_op jit(solution)/shard_map/pallas_call | solution.py:439
  80.7 0.7 copy.15
  81.4 0.6 copy.16
  82.0 0.6 copy.17
Async XLA Ops:
  0.6 0.9 %copy-start.5 = (s32[256]{0:T(256)S(1)}, s32[256]{0:T(256)}, u32[]{:S(2)}) copy-start(s32[256]{0:T(256)} %param.12) | copy-start | bytes 3076
  0.6 0.9 %copy-start.6 = (s32[2]{0:T(128)S(1)}, s32[2]{0:T(128)}, u32[]{:S(2)}) copy-start(s32[2]{0:T(128)} %bt_ref.1) | copy-start | bytes 28
  1.6 1.0 %copy-start = (bf16[1,64,4096]{2,1,0:T(8,128)(2,1)S(1)}, bf16[1,64,4096]{2,1,0:T(8,128)(2,1)}, u32[]{:S(2)}) copy-start(bf16[1,64,4096]{2,1,0:T(8,128)(2,1)} %b_ref.1) | copy-start | bytes 1572868
  2.6 0.9 %copy-start.1 = (bf16[256,512]{1,0:T(8,128)(2,1)S(1)}, bf16[256,512]{1,0:T(8,128)(2,1)}, u32[]{:S(2)}) copy-start(bf16[256,512]{1,0:T(8,128)(2,1)} %k_ref.1) | copy-start | bytes 786436
  3.6 0.9 %copy-start.2 = (bf16[256,512]{1,0:T(8,128)(2,1)S(1)}, bf16[256,512]{1,0:T(8,128)(2,1)}, u32[]{:S(2)}) copy-start(bf16[256,512]{1,0:T(8,128)(2,1)} %v_ref.1) | copy-start | bytes 786436
  4.5 0.9 %copy-start.3 = (bf16[256,256]{1,0:T(8,128)(2,1)S(1)}, bf16[256,256]{1,0:T(8,128)(2,1)}, u32[]{:S(2)}) copy-start(bf16[256,256]{1,0:T(8,128)(2,1)} %q_ref.1) | copy-start | bytes 393220
  5.4 0.9 %copy-start.4 = (bf16[256,256]{1,0:T(8,128)(2,1)S(1)}, bf16[256,256]{1,0:T(8,128)(2,1)}, u32[]{:S(2)}) copy-start(bf16[256,256]{1,0:T(8,128)(2,1)} %go_ref.1) | copy-start | bytes 393220

commit v2 on v1

v2 whole, which is shorter than its diff:
```python
import math

import jax
import jax.numpy as jnp
from jax import lax
from jax.experimental import pallas as pl
from jax.experimental.pallas import tpu as pltpu
from jax.sharding import PartitionSpec as P

HD = 128
RANK = 64
TOK = 256
NZ = 8
NX = 4
NYL = 4
N_CTX = 32
N_ADP = 16
SLOT = TOK + 16
HALF = TOK // 2
EXP2_SCALE = HD ** (-0.5) * math.log2(math.e)
FAR = -1e30
MESH = pl.DeviceIdType.MESH
F32 = jnp.float32
BF16 = jnp.bfloat16


def nt_dot(a, b):
    return lax.dot_general(a, b, (((1,), (1,)), ((), ())), preferred_element_type=F32)


def body(
    q_hbm, k_hbm, v_hbm, go_hbm, docs_hbm, bt_hbm, low_hbm, b_hbm,
    gq_hbm, glr_hbm, ga_hbm,
    kv, xkv, q_ref, go_ref, docs_ref, bt_ref, low_ref, gq_ref, glr_ref, ga_ref,
    acc, row_top, qdoc, bcols, btile, lowt, pbuf, qbuf, tbuf, gbuf, rsend, rbuf,
    loc_sem, mine_recv, other_recv, plus_send, minus_send, sib_send, sib2_send, x_send, y_send,
    bt_recv, bt_send, b_recv, b_send, bs_recv, bs_send,
    r_recv, r_send, p_recv, p_send, g_recv, g_send, out_sem,
):
    c = lax.axis_index("ctx")
    a = lax.axis_index("adp")
    core = c % 2
    pair = c // 2
    z = pair % NZ
    y_hi = pair // NZ
    head = a // NX
    x = a % NX
    mine = x % 2
    other = 1 - mine
    sib = pair * 2 + (1 - core)
    z_plus = (y_hi * NZ + (z + 1) % NZ) * 2 + core
    z_minus = (y_hi * NZ + (z + NZ - 1) % NZ) * 2 + core
    x_plus = head * NX + (x + 1) % NX
    x_minus = head * NX + (x + NX - 1) % NX
    y_ctx = ((1 - y_hi) * NZ + z) * 2 + core
    y_adp = (NYL - 1 - head) * NX + x
    selfdest = (pair == a).astype(jnp.int32)

    barrier = pltpu.get_barrier_semaphore()

    def greet(ctx, adp):
        pl.semaphore_signal(barrier, inc=1, device_id={"ctx": ctx, "adp": adp}, device_id_type=MESH)

    greet(y_ctx, y_adp)

    @pl.loop(1, N_CTX)
    def _(i):
        greet((c + i) % N_CTX, a)

    @pl.loop(1, N_ADP)
    def _(i):
        greet(c, (a + i) % N_ADP)

    @pl.loop(0, N_ADP)
    def _(i):
        @pl.when(jnp.logical_not((pair == a) & (i == pair)))
        def _():
            greet(i * 2 + core, pair)

    def col(which):
        return pl.ds(pl.multiple_of(which * HD, HD), HD)

    far_head = NYL - 1 - head
    get_docs = pltpu.make_async_copy(docs_hbm, docs_ref, loc_sem.at[0])
    own_k = pltpu.make_async_copy(k_hbm.at[:, col(head)], kv.at[c, 0, pl.ds(0, TOK)], loc_sem.at[1])
    own_v = pltpu.make_async_copy(v_hbm.at[:, col(head)], kv.at[c, 1, pl.ds(0, TOK)], loc_sem.at[2])
    x_k = pltpu.make_async_copy(k_hbm.at[:, col(far_head)], xkv.at[pl.ds(0, TOK)], loc_sem.at[3])
    x_v = pltpu.make_async_copy(v_hbm.at[:, col(far_head)], xkv.at[pl.ds(0, TOK)], loc_sem.at[3])
    get_q = pltpu.make_async_copy(q_hbm, q_ref, loc_sem.at[4])
    get_go = pltpu.make_async_copy(go_hbm, go_ref, loc_sem.at[5])
    get_bt = pltpu.make_async_copy(bt_hbm, bt_ref, loc_sem.at[6])
    get_low = pltpu.make_async_copy(low_hbm, low_ref, loc_sem.at[7])
    half = pl.multiple_of(core * (RANK // 2), RANK // 2)
    own_b = pltpu.make_async_copy(
        b_hbm.at[0, pl.ds(half, RANK // 2), pl.ds(pl.multiple_of(a * 2 * HD, 2 * HD), 2 * HD)],
        bcols.at[a, pl.ds(half, RANK // 2)],
        loc_sem.at[8],
    )
    get_docs.start()
    own_k.start()
    own_v.start()

    @pl.when(mine == 0)
    def _():
        x_k.start()

    @pl.when(mine == 1)
    def _():
        x_v.start()

    get_bt.start()
    get_q.start()
    get_go.start()
    get_low.start()
    own_b.start()

    get_docs.wait()
    doc_rows = docs_ref[...].astype(F32)
    tag = jnp.concatenate([doc_rows, jnp.zeros((14, HD), F32)], axis=0).astype(BF16)
    kv[c, mine, pl.ds(TOK, 16), :] = tag
    xkv[pl.ds(TOK, 16), :] = tag
    own_k.wait()
    own_v.wait()
    x_k.wait()
    pl.semaphore_wait(barrier, 1 + (N_CTX - 1) + (N_ADP - 1) + N_ADP - selfdest)

    def along(chunk, send_sem, to):
        ref = kv.at[chunk, mine]
        return pltpu.make_async_remote_copy(
            src_ref=ref, dst_ref=ref, send_sem=send_sem.at[chunk], recv_sem=mine_recv.at[chunk],
            device_id={"ctx": to, "adp": a}, device_id_type=MESH,
        )

    def rest_to_sib(chunk):
        ref = kv.at[chunk, other, pl.ds(0, TOK)]
        return pltpu.make_async_remote_copy(
            src_ref=ref, dst_ref=ref, send_sem=sib2_send.at[chunk], recv_sem=other_recv.at[chunk],
            device_id={"ctx": sib, "adp": a}, device_id_type=MESH,
        )

    def swap(chunk, first, to):
        ref = kv.at[chunk, mine, pl.ds(first, HALF)]
        return pltpu.make_async_remote_copy(
            src_ref=ref, dst_ref=ref, send_sem=x_send.at[chunk], recv_sem=other_recv.at[chunk],
            device_id={"ctx": c, "adp": to}, device_id_type=MESH,
        )

    def to_y():
        return pltpu.make_async_remote_copy(
            src_ref=xkv, dst_ref=kv.at[c, mine], send_sem=y_send, recv_sem=mine_recv.at[c],
            device_id={"ctx": y_ctx, "adp": y_adp}, device_id_type=MESH,
        )

    def await_mine(chunk):
        ref = kv.at[chunk, mine]
        pltpu.make_async_copy(ref, ref, mine_recv.at[chunk]).wait()

    def await_other(chunk):
        ref = kv.at[chunk, other, pl.ds(0, TOK)]
        pltpu.make_async_copy(ref, ref, other_recv.at[chunk]).wait()

    def await_swap_sent(chunk):
        ref = kv.at[chunk, mine, pl.ds(0, TOK)]
        pltpu.make_async_copy(ref, ref, x_send.at[chunk]).wait()

    along(c, plus_send, z_plus).start()
    along(c, minus_send, z_minus).start()

    @pl.when(y_hi == 0)
    def _():
        to_y().start()

    along(c, sib_send, sib).start()
    rest_to_sib(c).start()

    def b_copy(i):
        to = (a + i) % N_ADP
        return pltpu.make_async_remote_copy(
            src_ref=b_hbm.at[0, pl.ds(half, RANK // 2), pl.ds(pl.multiple_of(to * 2 * HD, 2 * HD), 2 * HD)],
            dst_ref=bcols.at[a, pl.ds(half, RANK // 2)],
            send_sem=b_send, recv_sem=b_recv,
            device_id={"ctx": c, "adp": to}, device_id_type=MESH,
        )

    def b_all(sem):
        ref = bcols.at[pl.ds(0, N_ADP - 1), pl.ds(half, RANK // 2)]
        return pltpu.make_async_copy(ref, ref, sem)

    def b_share():
        ref = bcols.at[:, pl.ds(half, RANK // 2)]
        return pltpu.make_async_remote_copy(
            src_ref=ref, dst_ref=ref, send_sem=bs_send, recv_sem=bs_recv,
            device_id={"ctx": sib, "adp": a}, device_id_type=MESH,
        )

    def b_shared():
        ref = bcols.at[:, pl.ds(pl.multiple_of((1 - core) * (RANK // 2), RANK // 2), RANK // 2)]
        return pltpu.make_async_copy(ref, ref, bs_recv)

    @pl.loop(1, N_ADP)
    def _(i):
        b_copy(i).start()

    get_bt.wait()
    btile[c] = jnp.where(lax.broadcasted_iota(jnp.int32, (2, HD), 0) == 0, bt_ref[0], bt_ref[1])

    def bt_copy(i):
        to = (c + i) % N_CTX
        return pltpu.make_async_remote_copy(
            src_ref=btile.at[c], dst_ref=btile.at[c], send_sem=bt_send, recv_sem=bt_recv,
            device_id={"ctx": to, "adp": a}, device_id_type=MESH,
        )

    def bt_all(sem):
        ref = btile.at[pl.ds(0, N_CTX - 1)]
        return pltpu.make_async_copy(ref, ref, sem)

    @pl.loop(1, N_CTX)
    def _(i):
        bt_copy(i).start()

    get_low.wait()
    rr = lax.broadcasted_iota(jnp.int32, (2 * RANK, RANK), 0)
    kk = lax.broadcasted_iota(jnp.int32, (2 * RANK, RANK), 1)
    pick = jnp.where(kk == ((rr >> 3) * 4 + (rr & 3)), 1.0, 0.0).astype(BF16)
    spread = jnp.dot(pick, low_ref[...], preferred_element_type=F32)
    rr = lax.broadcasted_iota(jnp.int32, (2 * RANK, TOK), 0)
    tt = lax.broadcasted_iota(jnp.int32, (2 * RANK, TOK), 1)
    lowt[...] = jnp.where((tt >> 7) == ((rr >> 2) & 1), spread, 0.0).astype(BF16)

    ri = lax.broadcasted_iota(jnp.int32, (HD, HD), 0)
    ci = lax.broadcasted_iota(jnp.int32, (HD, HD), 1)
    for part in range(2):
        spot = jnp.where(ri == ci, jnp.broadcast_to(doc_rows[part : part + 1, :], (HD, HD)), 0.0)
        column = jnp.sum(spot, axis=1, keepdims=True)
        qdoc[pl.ds(part * HD, HD), :] = jnp.broadcast_to(column, (HD, HD))

    ones = jnp.ones((TOK, HD), BF16)

    def attend(which, first):
        low_slot = which * 2
        row_doc = qdoc[...]
        for h in range(2):
            q_h = q_ref[:, h * HD : (h + 1) * HD]
            g_h = go_ref[:, h * HD : (h + 1) * HD]
            tiles = []
            for half_pair in range(2):
                scores = nt_dot(q_h, kv[low_slot + half_pair, 0, pl.ds(0, TOK), :])
                key_doc = kv[low_slot + half_pair, mine, pl.ds(TOK, 16), :].astype(F32)
                for lt in range(2):
                    seen = row_doc == key_doc[lt : lt + 1, :]
                    if first:
                        rpos = lax.broadcasted_iota(jnp.int32, (TOK, HD), 0) + core * TOK
                        kpos = lax.broadcasted_iota(jnp.int32, (TOK, HD), 1) + (half_pair * TOK + lt * HD)
                        seen = seen & (kpos <= rpos)
                    tiles.append(jnp.where(seen, scores[:, lt * HD : (lt + 1) * HD], FAR))
            top = jnp.maximum(jnp.maximum(tiles[0], tiles[1]), jnp.maximum(tiles[2], tiles[3]))
            top = jnp.broadcast_to(jnp.max(top, axis=1, keepdims=True), (TOK, HD))
            if not first:
                before = row_top[h]
                top = jnp.maximum(top, before)
                decay = jnp.exp2((before - top) * EXP2_SCALE)
            row_top[h] = top
            total = None
            for half_pair in range(2):
                weights = [
                    jnp.exp2((tiles[half_pair * 2 + lt] - top) * EXP2_SCALE) for lt in range(2)
                ]
                weights = jnp.concatenate(weights, axis=1)
                gw = nt_dot(g_h, kv[low_slot + half_pair, 1, pl.ds(0, TOK), :])
                both = jnp.concatenate([weights.astype(BF16), (weights * gw).astype(BF16)], axis=0)
                right = jnp.concatenate([kv[low_slot + half_pair, 0, pl.ds(0, TOK), :], ones], axis=1)
                term = jnp.dot(both, right, preferred_element_type=F32)
                total = term if total is None else total + term
            if first:
                acc[h] = total
            else:
                wide = jnp.concatenate([decay, decay], axis=1)
                wide = jnp.concatenate([wide, wide], axis=0)
                acc[h] = acc[h] * wide + total

    get_q.wait()
    get_go.wait()
    await_mine(sib)
    await_other(sib)
    attend(pair, True)

    def event(e):
        s, u = e // 4, e % 4
        lower, back = u // 2, u % 2
        dist = s - lower
        valid = (dist >= 0) & (lower <= y_hi)
        valid = valid & ((dist > 0) | ((lower == 1) & (back == 0)))
        valid = valid & ((dist <= 3) | ((dist == 4) & (back != lower)))
        from_z = (z + NZ - dist + 2 * dist * back) % NZ
        src_pair = jnp.where(lower == 1, 0, y_hi) * NZ + from_z
        on_plus = valid & ((back == 0) | (dist == 0)) & ((dist <= 2) | ((dist == 3) & (lower == 1)))
        on_minus = valid & ((back == 1) | (dist == 0)) & ((dist <= 2) | ((dist == 3) & (lower == 0)))
        return valid, src_pair, on_plus, on_minus

    @pl.loop(4, 25)
    def _(e):
        valid, src_pair, on_plus, on_minus = event(e)
        chunk = src_pair * 2 + core

        @pl.when(valid)
        def _():
            await_mine(chunk)

            @pl.when(on_plus)
            def _():
                along(chunk, plus_send, z_plus).start()

            @pl.when(on_minus)
            def _():
                along(chunk, minus_send, z_minus).start()

            swap(chunk, 0, x_plus).start()
            swap(chunk, HALF, x_minus).start()
            along(chunk, sib_send, sib).start()

        ready, src_pair, _, _ = event(e - 1)
        chunk2 = src_pair * 2 + core

        @pl.when(ready)
        def _():
            await_other(chunk2)
            rest_to_sib(chunk2).start()

        whole, last_pair, _, _ = event(e - 2)

        @pl.when(whole)
        def _():
            await_mine(last_pair * 2 + 1 - core)
            await_other(last_pair * 2 + 1 - core)

        @pl.when(whole & (last_pair < pair))
        def _():
            attend(last_pair, False)

    b_all(b_recv).wait()
    own_b.wait()
    b_share().start()

    for h in range(2):
        total = acc[h, pl.ds(0, TOK), pl.ds(HD, HD)]
        inv = 1.0 / total
        delta = acc[h, pl.ds(TOK, TOK), pl.ds(HD, HD)] * inv
        grad = (acc[h, pl.ds(TOK, TOK), pl.ds(0, HD)] - delta * acc[h, pl.ds(0, TOK), pl.ds(0, HD)]) * inv
        gq_ref[:, h * HD : (h + 1) * HD] = (grad * HD ** (-0.5)).astype(BF16)

    gq = gq_ref[...]
    partial = jnp.dot(lowt[...], gq, preferred_element_type=F32) * 2.0
    for h in range(2):
        pbuf[h] = partial[:, h * HD : (h + 1) * HD].reshape(N_ADP, 8, HD)

    def p_copy(i):
        to = (c + i) % N_CTX
        return pltpu.make_async_remote_copy(
            src_ref=pbuf.at[to % 2, to // 2], dst_ref=qbuf.at[c],
            send_sem=p_send, recv_sem=p_recv,
            device_id={"ctx": to, "adp": a}, device_id_type=MESH,
        )

    def p_all(sem):
        ref = qbuf.at[pl.ds(0, N_CTX - 1)]
        return pltpu.make_async_copy(ref, ref, sem)

    @pl.loop(1, N_CTX)
    def _(i):
        p_copy(i).start()

    qbuf[c] = pbuf[core, pair]
    out_gq = pltpu.make_async_copy(gq_ref, gq_hbm, out_sem.at[0])
    out_gq.start()

    b_shared().wait()
    for blk in range(2):
        chosen = bcols[bt_ref[blk]]
        padded = jnp.concatenate([chosen, jnp.zeros_like(chosen)], axis=0)
        part = nt_dot(gq[blk * HD : (blk + 1) * HD, :], padded) * 2.0
        rsend[pl.ds(blk * 8, 8)] = part.reshape(8, 16, HD)

    def r_copy(i):
        to = (a + i) % N_ADP
        return pltpu.make_async_remote_copy(
            src_ref=rsend.at[to], dst_ref=rbuf.at[a], send_sem=r_send, recv_sem=r_recv,
            device_id={"ctx": c, "adp": to}, device_id_type=MESH,
        )

    def r_all(sem):
        ref = rbuf.at[pl.ds(0, N_ADP - 1)]
        return pltpu.make_async_copy(ref, ref, sem)

    @pl.loop(1, N_ADP)
    def _(i):
        r_copy(i).start()

    rbuf[a] = rsend[a]

    bt_all(bt_recv).wait()
    bt_all(bt_send).wait()
    b_all(b_send).wait()
    b_share().wait_send()
    along(c, plus_send, z_plus).wait_send()
    along(c, minus_send, z_minus).wait_send()
    along(c, sib_send, sib).wait_send()
    rest_to_sib(c).wait_send()

    @pl.when(y_hi == 0)
    def _():
        to_y().wait_send()

    @pl.loop(4, 24)
    def _(e):
        valid, src_pair, on_plus, on_minus = event(e)
        chunk = src_pair * 2 + core

        @pl.when(on_plus)
        def _():
            along(chunk, plus_send, z_plus).wait_send()

        @pl.when(on_minus)
        def _():
            along(chunk, minus_send, z_minus).wait_send()

        @pl.when(valid)
        def _():
            await_swap_sent(chunk)
            along(chunk, sib_send, sib).wait_send()
            rest_to_sib(chunk).wait_send()

    p_all(p_recv).wait()
    upper = lax.broadcasted_iota(jnp.int32, (8, HD), 0) < 4

    def add_source(i, sums):
        tile = qbuf[i]
        owner = jnp.where(
            upper, jnp.broadcast_to(btile[i, 0:1, :], (8, HD)), jnp.broadcast_to(btile[i, 1:2, :], (8, HD))
        )
        return tuple(s + jnp.where(owner == t, tile, 0.0) for t, s in enumerate(sums))

    sums = lax.fori_loop(0, N_CTX, add_source, tuple(jnp.zeros((8, HD), F32) for _ in range(N_ADP)))
    for t in range(N_ADP):
        tbuf[t] = sums[t]

    def g_copy(t):
        return pltpu.make_async_remote_copy(
            src_ref=tbuf.at[t], dst_ref=gbuf.at[pair], send_sem=g_send, recv_sem=g_recv,
            device_id={"ctx": a * 2 + core, "adp": t}, device_id_type=MESH,
        )

    def g_wait(sem):
        @pl.when(selfdest == 0)
        def _():
            pltpu.make_async_copy(gbuf, gbuf, sem).wait()

        @pl.when(selfdest == 1)
        def _():
            ref = gbuf.at[pl.ds(0, N_ADP - 1)]
            pltpu.make_async_copy(ref, ref, sem).wait()

    @pl.loop(0, N_ADP)
    def _(i):
        t = (a + i) % N_ADP

        @pl.when(jnp.logical_not((pair == a) & (t == a)))
        def _():
            g_copy(t).start()

    @pl.when(pair == a)
    def _():
        gbuf[pair] = tbuf[a]

    r_all(r_recv).wait()
    share = rbuf[0]
    for i in range(1, N_ADP):
        share = share + rbuf[i]
    glr_ref[...] = share[:, :RANK]
    out_glr = pltpu.make_async_copy(glr_ref, glr_hbm, out_sem.at[1])
    out_glr.start()
    p_all(p_send).wait()
    r_all(r_send).wait()
    out_gq.wait()

    g_wait(g_recv)
    for i in range(N_ADP):
        tile = gbuf[i]
        ga_ref[0, pl.ds(i * 4, 4), :] = tile[0:4] + tile[4:8]
    out_ga = pltpu.make_async_copy(ga_ref, ga_hbm, out_sem.at[2])
    out_ga.start()
    g_wait(g_send)
    out_glr.wait()
    out_ga.wait()


def on_device(queries, keys, values, grad_out, docs, block_tenant, low_rank, adapter_b):
    anywhere = pl.BlockSpec(memory_space=pl.ANY)
    dma = pltpu.SemaphoreType.DMA
    return pl.pallas_call(
        body,
        out_shape=(
            jax.ShapeDtypeStruct((TOK, 2 * HD), BF16),
            jax.ShapeDtypeStruct((16, RANK), F32),
            jax.ShapeDtypeStruct((1, RANK, HD), F32),
        ),
        in_specs=[anywhere] * 8,
        out_specs=(anywhere,) * 3,
        scratch_shapes=[
            pltpu.VMEM((N_CTX, 2, SLOT, HD), BF16),
            pltpu.VMEM((SLOT, HD), BF16),
            pltpu.VMEM((TOK, 2 * HD), BF16),
            pltpu.VMEM((TOK, 2 * HD), BF16),
            pltpu.VMEM((2, HD), jnp.int32),
            pltpu.SMEM((2,), jnp.int32),
            pltpu.VMEM((RANK, TOK), BF16),
            pltpu.VMEM((TOK, 2 * HD), BF16),
            pltpu.VMEM((16, RANK), F32),
            pltpu.VMEM((1, RANK, HD), F32),
            pltpu.VMEM((2, 2 * TOK, 2 * HD), F32),
            pltpu.VMEM((2, TOK, HD), F32),
            pltpu.VMEM((TOK, HD), F32),
            pltpu.VMEM((N_ADP, RANK, 2 * HD), BF16),
            pltpu.VMEM((N_CTX, 2, HD), jnp.int32),
            pltpu.VMEM((2 * RANK, TOK), BF16),
            pltpu.VMEM((2, N_ADP, 8, HD), F32),
            pltpu.VMEM((N_CTX, 8, HD), F32),
            pltpu.VMEM((N_ADP, 8, HD), F32),
            pltpu.VMEM((N_ADP, 8, HD), F32),
            pltpu.VMEM((N_ADP, 16, HD), F32),
            pltpu.VMEM((N_ADP, 16, HD), F32),
            dma((9,)), dma((N_CTX,)), dma((N_CTX,)), dma((N_CTX,)), dma((N_CTX,)),
            dma((N_CTX,)), dma((N_CTX,)), dma((N_CTX,)), dma,
            dma, dma, dma, dma, dma, dma, dma, dma, dma, dma, dma, dma, dma((3,)),
        ],
        compiler_params=pltpu.CompilerParams(
            collective_id=0, has_side_effects=True, vmem_limit_bytes=60 * 1024 * 1024
        ),
        cost_estimate=pl.CostEstimate(flops=4_000_000_000, bytes_accessed=4_000_000, transcendentals=4_000_000),
    )(
        queries, keys, values, grad_out, docs.reshape(2, HD), block_tenant, low_rank.T, adapter_b
    )


def solution(mesh):
    placed = (
        P("ctx", "adp"),
        P("ctx", None),
        P("ctx", None),
        P("ctx", "adp"),
        P("ctx"),
        P("ctx"),
        P("ctx", None),
        P("adp", None, None),
    )
    return jax.shard_map(
        on_device,
        mesh=mesh,
        in_specs=placed,
        out_specs=(P("ctx", "adp"), P(("ctx", "adp"), None), P("adp", None, "ctx")),
        check_vma=False,
    )
```

time: 84 us -> 83.6 us (level)
  the two profiles are of different devices: /device:TPU:1 before, /device:TPU:112 now
where the time goes in v2:
time: 83.6 us; the launch traced here: 83.4 us
  Pallas kernels  80 us (96%)
  local copies, waits for them, and re-layouts  2.8 us (3%)
    pallas_call x1, Pallas kernels, on_device(): pl.pallas_call(body, out_shape=(jax.ShapeDtypeStruct((TOK, 2 * HD), BF16)...  80 us
    unnamed x7, local copies, waits for them, and re-layouts  2.8 us

profile of v2, /device:TPU:112, one launch (start us, length us, event | category | flops | bytes accessed | tf_op | source)
XLA Modules:
  0.0 83.4 jit_solution(3426488236557868743)
XLA Ops:
  0.6 80.0 %shard_map.103 = (bf16[256,256]{1,0:T(8,128)(2,1)}, f32[16,64]{1,0:T(8,128)}, f32[1,64,128]{2,1,0:T(8,128)}) custom-call(bf16[256,256]{1,0:T(8,128)(2,1)} %q_hbm.1, bf16[256,512]{1,0:T(8,128)(2,1)} %k_hbm.1, bf16[256,512]{1,0:T(8,128)(2,1)} %v_hbm.1, bf16[256,256]{1,0:T(8,128)(2,1)} %go_hbm.1, s32[2,128]{1,0:T(2,128)} %bitcast.3, s32[2]{0:T(128)} %bt_hbm.1, ...), custom_call_target="tpu_custom_call" | custom-call | flops 4000000000 | bytes 4000000 | tf_op jit(solution)/shard_map/pallas_call | solution.py:500
  80.6 0.0 copy-start.1
  80.6 0.0 copy-start
  80.6 1.6 %copy.14 = bf16[256,256]{1,0:T(8,128)(2,1)} copy(bf16[256,256]{1,0:T(8,128)(2,1)} %get-tuple-element.6) | data formatting | bytes 262144
  82.2 0.0 copy-done.1
  82.2 0.6 copy.15
  82.8 0.0 copy-done
  82.8 0.6 copy.16
Async XLA Ops:
  80.6 1.6 %copy-start.1 = (f32[16,64]{1,0:T(8,128)S(1)}, f32[16,64]{1,0:T(8,128)}, u32[]{:S(2)}) copy-start(f32[16,64]{1,0:T(8,128)} %get-tuple-element.7) | copy-start | bytes 12292
  80.6 2.2 %copy-start = (f32[1,64,128]{2,1,0:T(8,128)S(1)}, f32[1,64,128]{2,1,0:T(8,128)}, u32[]{:S(2)}) copy-start(f32[1,64,128]{2,1,0:T(8,128)} %get-tuple-element.8) | copy-start | bytes 98308

commit v3 on v2

--- a/solution.py
+++ b/solution.py
@@ -24,6 +24,14 @@
 BF16 = jnp.bfloat16
 
 
+def rem(value, by):
+    return lax.rem(value, jnp.int32(by))
+
+
+def div(value, by):
+    return lax.div(value, jnp.int32(by))
+
+
 def nt_dot(a, b):
     return lax.dot_general(a, b, (((1,), (1,)), ((), ())), preferred_element_type=F32)
 
@@ -32,26 +40,26 @@
     q_hbm, k_hbm, v_hbm, go_hbm, docs_hbm, bt_hbm, low_hbm, b_hbm,
     gq_hbm, glr_hbm, ga_hbm,
     kv, xkv, q_ref, go_ref, docs_ref, bt_ref, low_ref, gq_ref, glr_ref, ga_ref,
-    acc, row_top, qdoc, bcols, btile, lowt, pbuf, qbuf, tbuf, gbuf, rsend, rbuf,
+    acc, row_top, qdoc, bcols, bt_mine, btile, lowt, pbuf, qbuf, tbuf, gbuf, rsend, rbuf,
     loc_sem, mine_recv, other_recv, plus_send, minus_send, sib_send, sib2_send, x_send, y_send,
     bt_recv, bt_send, b_recv, b_send, bs_recv, bs_send,
     r_recv, r_send, p_recv, p_send, g_recv, g_send, out_sem,
 ):
     c = lax.axis_index("ctx")
     a = lax.axis_index("adp")
-    core = c % 2
-    pair = c // 2
-    z = pair % NZ
-    y_hi = pair // NZ
-    head = a // NX
-    x = a % NX
-    mine = x % 2
+    core = rem(c, 2)
+    pair = div(c, 2)
+    z = rem(pair, NZ)
+    y_hi = div(pair, NZ)
+    head = div(a, NX)
+    x = rem(a, NX)
+    mine = rem(x, 2)
     other = 1 - mine
     sib = pair * 2 + (1 - core)
-    z_plus = (y_hi * NZ + (z + 1) % NZ) * 2 + core
-    z_minus = (y_hi * NZ + (z + NZ - 1) % NZ) * 2 + core
-    x_plus = head * NX + (x + 1) % NX
-    x_minus = head * NX + (x + NX - 1) % NX
+    z_plus = (y_hi * NZ + rem(z + 1, NZ)) * 2 + core
+    z_minus = (y_hi * NZ + rem(z + NZ - 1, NZ)) * 2 + core
+    x_plus = head * NX + rem(x + 1, NX)
+    x_minus = head * NX + rem(x + NX - 1, NX)
     y_ctx = ((1 - y_hi) * NZ + z) * 2 + core
     y_adp = (NYL - 1 - head) * NX + x
     selfdest = (pair == a).astype(jnp.int32)
@@ -62,20 +70,19 @@
         pl.semaphore_signal(barrier, inc=1, device_id={"ctx": ctx, "adp": adp}, device_id_type=MESH)
 
     greet(y_ctx, y_adp)
-
-    @pl.loop(1, N_CTX)
-    def _(i):
-        greet((c + i) % N_CTX, a)
+    greet(z_plus, a)
+    greet(z_minus, a)
+    greet(sib, a)
 
     @pl.loop(1, N_ADP)
     def _(i):
-        greet(c, (a + i) % N_ADP)
-
-    @pl.loop(0, N_ADP)
+        greet(c, rem(a + i, N_ADP))
+
+    @pl.loop(0, N_CTX)
     def _(i):
-        @pl.when(jnp.logical_not((pair == a) & (i == pair)))
-        def _():
-            greet(i * 2 + core, pair)
+        @pl.when(jnp.logical_not((pair == a) & (i == c)))
+        def _():
+            greet(i, pair)
 
     def col(which):
         return pl.ds(pl.multiple_of(which * HD, HD), HD)
@@ -122,7 +129,7 @@
     own_k.wait()
     own_v.wait()
     x_k.wait()
-    pl.semaphore_wait(barrier, 1 + (N_CTX - 1) + (N_ADP - 1) + N_ADP - selfdest)
+    pl.semaphore_wait(barrier, 4 + (N_ADP - 1) + N_CTX - selfdest)
 
     def along(chunk, send_sem, to):
         ref = kv.at[chunk, mine]
@@ -174,7 +181,7 @@
     rest_to_sib(c).start()
 
     def b_copy(i):
-        to = (a + i) % N_ADP
+        to = rem(a + i, N_ADP)
         return pltpu.make_async_remote_copy(
             src_ref=b_hbm.at[0, pl.ds(half, RANK // 2), pl.ds(pl.multiple_of(to * 2 * HD, 2 * HD), 2 * HD)],
             dst_ref=bcols.at[a, pl.ds(half, RANK // 2)],
@@ -202,22 +209,40 @@
         b_copy(i).start()
 
     get_bt.wait()
-    btile[c] = jnp.where(lax.broadcasted_iota(jnp.int32, (2, HD), 0) == 0, bt_ref[0], bt_ref[1])
+    bt_mine[...] = jnp.where(lax.broadcasted_iota(jnp.int32, (2, HD), 0) == 0, bt_ref[0], bt_ref[1])
+
+    def to_sum(i):
+        return a * 2 + rem(i, 2), rem(a + div(i, 2), N_ADP)
 
     def bt_copy(i):
-        to = (c + i) % N_CTX
-        return pltpu.make_async_remote_copy(
-            src_ref=btile.at[c], dst_ref=btile.at[c], send_sem=bt_send, recv_sem=bt_recv,
-            device_id={"ctx": to, "adp": a}, device_id_type=MESH,
-        )
-
-    def bt_all(sem):
-        ref = btile.at[pl.ds(0, N_CTX - 1)]
-        return pltpu.make_async_copy(ref, ref, sem)
-
-    @pl.loop(1, N_CTX)
+        ctx, adp = to_sum(i)
+        return pltpu.make_async_remote_copy(
+            src_ref=bt_mine, dst_ref=btile.at[c], send_sem=bt_send, recv_sem=bt_recv,
+            device_id={"ctx": ctx, "adp": adp}, device_id_type=MESH,
+        )
+
+    def wait_all(buffer, sem):
+        @pl.when(selfdest == 0)
+        def _():
+            pltpu.make_async_copy(buffer, buffer, sem).wait()
+
+        @pl.when(selfdest == 1)
+        def _():
+            ref = buffer.at[pl.ds(0, N_CTX - 1)]
+            pltpu.make_async_copy(ref, ref, sem).wait()
+
+    def is_self(i):
+        return (selfdest == 1) & (i == core)
+
+    @pl.loop(0, N_CTX)
     def _(i):
-        bt_copy(i).start()
+        @pl.when(jnp.logical_not(is_self(i)))
+        def _():
+            bt_copy(i).start()
+
+    @pl.when(selfdest == 1)
+    def _():
+        btile[c] = bt_mine[...]
 
     get_low.wait()
     rr = lax.broadcasted_iota(jnp.int32, (2 * RANK, RANK), 0)
@@ -286,19 +311,21 @@
     attend(pair, True)
 
     def event(e):
-        s, u = e // 4, e % 4
-        lower, back = u // 2, u % 2
+        late = e >= 4
+        e = jnp.maximum(e, 0)
+        s, u = div(e, 4), rem(e, 4)
+        lower, back = div(u, 2), rem(u, 2)
         dist = s - lower
-        valid = (dist >= 0) & (lower <= y_hi)
+        valid = late & (dist >= 0) & (lower <= y_hi)
         valid = valid & ((dist > 0) | ((lower == 1) & (back == 0)))
         valid = valid & ((dist <= 3) | ((dist == 4) & (back != lower)))
-        from_z = (z + NZ - dist + 2 * dist * back) % NZ
-        src_pair = jnp.where(lower == 1, 0, y_hi) * NZ + from_z
+        from_z = rem(z + NZ + dist * (2 * back - 1), NZ)
+        src_pair = (y_hi - y_hi * lower) * NZ + from_z
         on_plus = valid & ((back == 0) | (dist == 0)) & ((dist <= 2) | ((dist == 3) & (lower == 1)))
         on_minus = valid & ((back == 1) | (dist == 0)) & ((dist <= 2) | ((dist == 3) & (lower == 0)))
         return valid, src_pair, on_plus, on_minus
 
-    @pl.loop(4, 25)
+    @pl.loop(4, 28)
     def _(e):
         valid, src_pair, on_plus, on_minus = event(e)
         chunk = src_pair * 2 + core
@@ -319,7 +346,7 @@
             swap(chunk, HALF, x_minus).start()
             along(chunk, sib_send, sib).start()
 
-        ready, src_pair, _, _ = event(e - 1)
+        ready, src_pair, _, _ = event(e - 3)
         chunk2 = src_pair * 2 + core
 
         @pl.when(ready)
@@ -327,7 +354,7 @@
             await_other(chunk2)
             rest_to_sib(chunk2).start()
 
-        whole, last_pair, _, _ = event(e - 2)
+        whole, last_pair, _, _ = event(e - 5)
 
         @pl.when(whole)
         def _():
@@ -355,22 +382,23 @@
         pbuf[h] = partial[:, h * HD : (h + 1) * HD].reshape(N_ADP, 8, HD)
 
     def p_copy(i):
-        to = (c + i) % N_CTX
-        return pltpu.make_async_remote_copy(
-            src_ref=pbuf.at[to % 2, to // 2], dst_ref=qbuf.at[c],
+        ctx, adp = to_sum(i)
+        return pltpu.make_async_remote_copy(
+            src_ref=pbuf.at[rem(i, 2), adp], dst_ref=qbuf.at[c],
             send_sem=p_send, recv_sem=p_recv,
-            device_id={"ctx": to, "adp": a}, device_id_type=MESH,
-        )
-
-    def p_all(sem):
-        ref = qbuf.at[pl.ds(0, N_CTX - 1)]
-        return pltpu.make_async_copy(ref, ref, sem)
-
-    @pl.loop(1, N_CTX)
+            device_id={"ctx": ctx, "adp": adp}, device_id_type=MESH,
+        )
+
+    @pl.loop(0, N_CTX)
     def _(i):
-        p_copy(i).start()
-
-    qbuf[c] = pbuf[core, pair]
+        @pl.when(jnp.logical_not(is_self(i)))
+        def _():
+            p_copy(i).start()
+
+    @pl.when(selfdest == 1)
+    def _():
+        qbuf[c] = pbuf[core, a]
+
     out_gq = pltpu.make_async_copy(gq_ref, gq_hbm, out_sem.at[0])
     out_gq.start()
 
@@ -382,7 +410,7 @@
         rsend[pl.ds(blk * 8, 8)] = part.reshape(8, 16, HD)
 
     def r_copy(i):
-        to = (a + i) % N_ADP
+        to = rem(a + i, N_ADP)
         return pltpu.make_async_remote_copy(
             src_ref=rsend.at[to], dst_ref=rbuf.at[a], send_sem=r_send, recv_sem=r_recv,
             device_id={"ctx": c, "adp": to}, device_id_type=MESH,
@@ -398,8 +426,8 @@
 
     rbuf[a] = rsend[a]
 
-    bt_all(bt_recv).wait()
-    bt_all(bt_send).wait()
+    wait_all(btile, bt_recv)
+    wait_all(btile, bt_send)
     b_all(b_send).wait()
     b_share().wait_send()
     along(c, plus_send, z_plus).wait_send()
@@ -430,7 +458,7 @@
             along(chunk, sib_send, sib).wait_send()
             rest_to_sib(chunk).wait_send()
 
-    p_all(p_recv).wait()
+    wait_all(qbuf, p_recv)
     upper = lax.broadcasted_iota(jnp.int32, (8, HD), 0) < 4
 
     def add_source(i, sums):
@@ -444,33 +472,22 @@
     for t in range(N_ADP):
         tbuf[t] = sums[t]
 
-    def g_copy(t):
-        return pltpu.make_async_remote_copy(
-            src_ref=tbuf.at[t], dst_ref=gbuf.at[pair], send_sem=g_send, recv_sem=g_recv,
-            device_id={"ctx": a * 2 + core, "adp": t}, device_id_type=MESH,
-        )
-
-    def g_wait(sem):
-        @pl.when(selfdest == 0)
-        def _():
-            pltpu.make_async_copy(gbuf, gbuf, sem).wait()
-
-        @pl.when(selfdest == 1)
-        def _():
-            ref = gbuf.at[pl.ds(0, N_ADP - 1)]
-            pltpu.make_async_copy(ref, ref, sem).wait()
-
-    @pl.loop(0, N_ADP)
+    def g_copy(i):
+        to = rem(a + i, N_ADP)
+        return pltpu.make_async_remote_copy(
+            src_ref=tbuf.at[to], dst_ref=gbuf.at[a], send_sem=g_send, recv_sem=g_recv,
+            device_id={"ctx": c, "adp": to}, device_id_type=MESH,
+        )
+
+    def g_all(sem):
+        ref = gbuf.at[pl.ds(0, N_ADP - 1)]
+        return pltpu.make_async_copy(ref, ref, sem)
+
+    @pl.loop(1, N_ADP)
     def _(i):
-        t = (a + i) % N_ADP
-
-        @pl.when(jnp.logical_not((pair == a) & (t == a)))
-        def _():
-            g_copy(t).start()
-
-    @pl.when(pair == a)
-    def _():
-        gbuf[pair] = tbuf[a]
+        g_copy(i).start()
+
+    gbuf[a] = tbuf[a]
 
     r_all(r_recv).wait()
     share = rbuf[0]
@@ -479,31 +496,44 @@
     glr_ref[...] = share[:, :RANK]
     out_glr = pltpu.make_async_copy(glr_ref, glr_hbm, out_sem.at[1])
     out_glr.start()
-    p_all(p_send).wait()
+    wait_all(qbuf, p_send)
     r_all(r_send).wait()
     out_gq.wait()
 
-    g_wait(g_recv)
+    g_all(g_recv).wait()
     for i in range(N_ADP):
         tile = gbuf[i]
         ga_ref[0, pl.ds(i * 4, 4), :] = tile[0:4] + tile[4:8]
     out_ga = pltpu.make_async_copy(ga_ref, ga_hbm, out_sem.at[2])
     out_ga.start()
-    g_wait(g_send)
+    g_all(g_send).wait()
     out_glr.wait()
     out_ga.wait()
+
+
+def finish(gq_in, glr_in, ga_in, gq_out, glr_out, ga_out, sems):
+    copies = [
+        pltpu.make_async_copy(gq_in, gq_out, sems.at[0]),
+        pltpu.make_async_copy(glr_in, glr_out, sems.at[1]),
+        pltpu.make_async_copy(ga_in, ga_out, sems.at[2]),
+    ]
+    for copy in copies:
+        copy.start()
+    for copy in copies:
+        copy.wait()
 
 
 def on_device(queries, keys, values, grad_out, docs, block_tenant, low_rank, adapter_b):
     anywhere = pl.BlockSpec(memory_space=pl.ANY)
     dma = pltpu.SemaphoreType.DMA
-    return pl.pallas_call(
+    shapes = (
+        jax.ShapeDtypeStruct((TOK, 2 * HD), BF16),
+        jax.ShapeDtypeStruct((16, RANK), F32),
+        jax.ShapeDtypeStruct((1, RANK, HD), F32),
+    )
+    grads = pl.pallas_call(
         body,
-        out_shape=(
-            jax.ShapeDtypeStruct((TOK, 2 * HD), BF16),
-            jax.ShapeDtypeStruct((16, RANK), F32),
-            jax.ShapeDtypeStruct((1, RANK, HD), F32),
-        ),
+        out_shape=shapes,
         in_specs=[anywhere] * 8,
         out_specs=(anywhere,) * 3,
         scratch_shapes=[
@@ -521,6 +551,7 @@
             pltpu.VMEM((2, TOK, HD), F32),
             pltpu.VMEM((TOK, HD), F32),
             pltpu.VMEM((N_ADP, RANK, 2 * HD), BF16),
+            pltpu.VMEM((2, HD), jnp.int32),
             pltpu.VMEM((N_CTX, 2, HD), jnp.int32),
             pltpu.VMEM((2 * RANK, TOK), BF16),
             pltpu.VMEM((2, N_ADP, 8, HD), F32),
@@ -540,6 +571,14 @@
     )(
         queries, keys, values, grad_out, docs.reshape(2, HD), block_tenant, low_rank.T, adapter_b
     )
+    return pl.pallas_call(
+        finish,
+        out_shape=shapes,
+        in_specs=[anywhere] * 3,
+        out_specs=(anywhere,) * 3,
+        scratch_shapes=[dma((3,))],
+        compiler_params=pltpu.CompilerParams(vmem_limit_bytes=60 * 1024 * 1024),
+    )(*grads)
 
 
 def solution(mesh):

time: 83.6 us -> 70.8 us (0.85)
  the two profiles are of different devices: /device:TPU:112 before, /device:TPU:1 now
where the time goes in v3:
time: 70.8 us; the launch traced here: 70.7 us
  Pallas kernels  70.1 us (99%)
    pallas_call x1, Pallas kernels, on_device(): pl.pallas_call(body, out_shape=shapes, in_specs=[anywhere] * 8, out_specs...  63.7 us
    pallas_call x1, Pallas kernels, on_device(): pl.pallas_call(finish, out_shape=shapes, in_specs=[anywhere] * 3, out_spe...  6.34 us

profile of v3, /device:TPU:1, one launch (start us, length us, event | category | flops | bytes accessed | tf_op | source)
XLA Modules:
  0.0 70.7 jit_solution(7218664628739388509)
XLA Ops:
  0.6 63.7 %shard_map.103 = (bf16[256,256]{1,0:T(8,128)(2,1)}, f32[16,64]{1,0:T(8,128)}, f32[1,64,128]{2,1,0:T(8,128)}) custom-call(bf16[256,256]{1,0:T(8,128)(2,1)} %q_hbm.1, bf16[256,512]{1,0:T(8,128)(2,1)} %k_hbm.1, bf16[256,512]{1,0:T(8,128)(2,1)} %v_hbm.1, bf16[256,256]{1,0:T(8,128)(2,1)} %go_hbm.1, s32[2,128]{1,0:T(2,128)} %bitcast.3, s32[2]{0:T(128)} %bt_hbm.1, ...), custom_call_target="tpu_custom_call" | custom-call | flops 4000000000 | bytes 4000000 | tf_op jit(solution)/shard_map/pallas_call | solution.py:534
  64.4 6.3 %shard_map.104 = (bf16[256,256]{1,0:T(8,128)(2,1)}, f32[16,64]{1,0:T(8,128)}, f32[1,64,128]{2,1,0:T(8,128)}) custom-call(bf16[256,256]{1,0:T(8,128)(2,1)} %get-tuple-element.6.gq_in, f32[16,64]{1,0:T(8,128)} %get-tuple-element.7.glr_in, f32[1,64,128]{2,1,0:T(8,128)} %get-tuple-element.8.ga_in), custom_call_target="tpu_custom_call" | custom-call | tf_op jit(solution)/shard_map/pallas_call | solution.py:574

commit v4 on v3

--- a/solution.py
+++ b/solution.py
@@ -20,6 +20,11 @@
 EXP2_SCALE = HD ** (-0.5) * math.log2(math.e)
 FAR = -1e30
 MESH = pl.DeviceIdType.MESH
+ARRIVALS = (1, 7, 3, 5, 8 + 0, 8 + 3, 8 + 5, 2, 6, 4, 8 + 1, 8 + 7, 8 + 2, 8 + 6, 8 + 4)
+EARLY = sum(code << (4 * i) for i, code in enumerate(ARRIVALS[:7]))
+LATE = sum(code << (4 * i) for i, code in enumerate(ARRIVALS[7:14]))
+LAST = ARRIVALS[14]
+LAG_SWAP, LAG_USE = 3, 5
 F32 = jnp.float32
 BF16 = jnp.bfloat16
 
@@ -41,7 +46,7 @@
     gq_hbm, glr_hbm, ga_hbm,
     kv, xkv, q_ref, go_ref, docs_ref, bt_ref, low_ref, gq_ref, glr_ref, ga_ref,
     acc, row_top, qdoc, bcols, bt_mine, btile, lowt, pbuf, qbuf, tbuf, gbuf, rsend, rbuf,
-    loc_sem, mine_recv, other_recv, plus_send, minus_send, sib_send, sib2_send, x_send, y_send,
+    loc_sem, mine_recv, other_recv, plus_send, minus_send, sib_send, sib2_send, x_send, y_send, far_send,
     bt_recv, bt_send, b_recv, b_send, bs_recv, bs_send,
     r_recv, r_send, p_recv, p_send, g_recv, g_send, out_sem,
 ):
@@ -58,9 +63,14 @@
     sib = pair * 2 + (1 - core)
     z_plus = (y_hi * NZ + rem(z + 1, NZ)) * 2 + core
     z_minus = (y_hi * NZ + rem(z + NZ - 1, NZ)) * 2 + core
+    z_plus3 = (y_hi * NZ + rem(z + 3, NZ)) * 2 + core
+    z_minus3 = (y_hi * NZ + rem(z + NZ - 3, NZ)) * 2 + core
     x_plus = head * NX + rem(x + 1, NX)
     x_minus = head * NX + rem(x + NX - 1, NX)
-    y_ctx = ((1 - y_hi) * NZ + z) * 2 + core
+
+    def y_ctx(step):
+        return ((1 - y_hi) * NZ + rem(z + NZ + step, NZ)) * 2 + core
+
     y_adp = (NYL - 1 - head) * NX + x
     selfdest = (pair == a).astype(jnp.int32)
 
@@ -69,10 +79,16 @@
     def greet(ctx, adp):
         pl.semaphore_signal(barrier, inc=1, device_id={"ctx": ctx, "adp": adp}, device_id_type=MESH)
 
-    greet(y_ctx, y_adp)
     greet(z_plus, a)
     greet(z_minus, a)
+    greet(z_plus3, a)
+    greet(z_minus3, a)
     greet(sib, a)
+
+    @pl.when(y_hi == 1)
+    def _():
+        for step in (0, 3, -3):
+            greet(y_ctx(step), y_adp)
 
     @pl.loop(1, N_ADP)
     def _(i):
@@ -129,7 +145,7 @@
     own_k.wait()
     own_v.wait()
     x_k.wait()
-    pl.semaphore_wait(barrier, 4 + (N_ADP - 1) + N_CTX - selfdest)
+    pl.semaphore_wait(barrier, 5 + 3 * (1 - y_hi) + (N_ADP - 1) + N_CTX - selfdest)
 
     def along(chunk, send_sem, to):
         ref = kv.at[chunk, mine]
@@ -152,10 +168,17 @@
             device_id={"ctx": c, "adp": to}, device_id_type=MESH,
         )
 
-    def to_y():
-        return pltpu.make_async_remote_copy(
-            src_ref=xkv, dst_ref=kv.at[c, mine], send_sem=y_send, recv_sem=mine_recv.at[c],
-            device_id={"ctx": y_ctx, "adp": y_adp}, device_id_type=MESH,
+    def to_y(which):
+        return pltpu.make_async_remote_copy(
+            src_ref=xkv, dst_ref=kv.at[c, mine], send_sem=y_send.at[which], recv_sem=mine_recv.at[c],
+            device_id={"ctx": y_ctx((0, 3, -3)[which]), "adp": y_adp}, device_id_type=MESH,
+        )
+
+    def far(which):
+        ref = kv.at[c, mine]
+        return pltpu.make_async_remote_copy(
+            src_ref=ref, dst_ref=ref, send_sem=far_send.at[which], recv_sem=mine_recv.at[c],
+            device_id={"ctx": (z_plus3, z_minus3)[which], "adp": a}, device_id_type=MESH,
         )
 
     def await_mine(chunk):
@@ -173,9 +196,13 @@
     along(c, plus_send, z_plus).start()
     along(c, minus_send, z_minus).start()
 
+    far(0).start()
+    far(1).start()
+
     @pl.when(y_hi == 0)
     def _():
-        to_y().start()
+        for which in range(3):
+            to_y(which).start()
 
     along(c, sib_send, sib).start()
     rest_to_sib(c).start()
@@ -311,21 +338,21 @@
     attend(pair, True)
 
     def event(e):
-        late = e >= 4
-        e = jnp.maximum(e, 0)
-        s, u = div(e, 4), rem(e, 4)
-        lower, back = div(u, 2), rem(u, 2)
-        dist = s - lower
-        valid = late & (dist >= 0) & (lower <= y_hi)
-        valid = valid & ((dist > 0) | ((lower == 1) & (back == 0)))
-        valid = valid & ((dist <= 3) | ((dist == 4) & (back != lower)))
-        from_z = rem(z + NZ + dist * (2 * back - 1), NZ)
-        src_pair = (y_hi - y_hi * lower) * NZ + from_z
-        on_plus = valid & ((back == 0) | (dist == 0)) & ((dist <= 2) | ((dist == 3) & (lower == 1)))
-        on_minus = valid & ((back == 1) | (dist == 0)) & ((dist <= 2) | ((dist == 3) & (lower == 0)))
+        e_low = jnp.clip(e, 0, 6)
+        e_high = jnp.clip(e - 7, 0, 6)
+        code = jnp.where(
+            e < 7, lax.shift_right_logical(jnp.int32(EARLY), 4 * e_low),
+            jnp.where(e < 14, lax.shift_right_logical(jnp.int32(LATE), 4 * e_high), LAST),
+        )
+        code = code & 15
+        lower, off = div(code, 8), rem(code, 8)
+        valid = (e >= 0) & (e < len(ARRIVALS)) & (lower <= y_hi)
+        src_pair = (y_hi - lower) * NZ + rem(z + NZ - off, NZ)
+        on_plus = valid & ((off == 0) | (off == 5) | ((off == 3) & (lower == 1)))
+        on_minus = valid & ((off == 0) | (off == 3) | ((off == 5) & (lower == 0)))
         return valid, src_pair, on_plus, on_minus
 
-    @pl.loop(4, 28)
+    @pl.loop(0, len(ARRIVALS) + LAG_USE)
     def _(e):
         valid, src_pair, on_plus, on_minus = event(e)
         chunk = src_pair * 2 + core
@@ -346,7 +373,7 @@
             swap(chunk, HALF, x_minus).start()
             along(chunk, sib_send, sib).start()
 
-        ready, src_pair, _, _ = event(e - 3)
+        ready, src_pair, _, _ = event(e - LAG_SWAP)
         chunk2 = src_pair * 2 + core
 
         @pl.when(ready)
@@ -354,7 +381,7 @@
             await_other(chunk2)
             rest_to_sib(chunk2).start()
 
-        whole, last_pair, _, _ = event(e - 5)
+        whole, last_pair, _, _ = event(e - LAG_USE)
 
         @pl.when(whole)
         def _():
@@ -435,11 +462,15 @@
     along(c, sib_send, sib).wait_send()
     rest_to_sib(c).wait_send()
 
+    far(0).wait_send()
+    far(1).wait_send()
+
     @pl.when(y_hi == 0)
     def _():
-        to_y().wait_send()
-
-    @pl.loop(4, 24)
+        for which in range(3):
+            to_y(which).wait_send()
+
+    @pl.loop(0, len(ARRIVALS))
     def _(e):
         valid, src_pair, on_plus, on_minus = event(e)
         chunk = src_pair * 2 + core
@@ -511,20 +542,15 @@
     out_ga.wait()
 
 
-def finish(gq_in, glr_in, ga_in, gq_out, glr_out, ga_out, sems):
-    copies = [
-        pltpu.make_async_copy(gq_in, gq_out, sems.at[0]),
-        pltpu.make_async_copy(glr_in, glr_out, sems.at[1]),
-        pltpu.make_async_copy(ga_in, ga_out, sems.at[2]),
-    ]
-    for copy in copies:
-        copy.start()
-    for copy in copies:
-        copy.wait()
+def finish(gq_in, glr_in, ga_in, gq_out, glr_out, ga_out):
+    gq_out[...] = gq_in[...]
+    glr_out[...] = glr_in[...]
+    ga_out[...] = ga_in[...]
 
 
 def on_device(queries, keys, values, grad_out, docs, block_tenant, low_rank, adapter_b):
     anywhere = pl.BlockSpec(memory_space=pl.ANY)
+    vmem = pl.BlockSpec(memory_space=pltpu.VMEM)
     dma = pltpu.SemaphoreType.DMA
     shapes = (
         jax.ShapeDtypeStruct((TOK, 2 * HD), BF16),
@@ -561,7 +587,7 @@
             pltpu.VMEM((N_ADP, 16, HD), F32),
             pltpu.VMEM((N_ADP, 16, HD), F32),
             dma((9,)), dma((N_CTX,)), dma((N_CTX,)), dma((N_CTX,)), dma((N_CTX,)),
-            dma((N_CTX,)), dma((N_CTX,)), dma((N_CTX,)), dma,
+            dma((N_CTX,)), dma((N_CTX,)), dma((N_CTX,)), dma((3,)), dma((2,)),
             dma, dma, dma, dma, dma, dma, dma, dma, dma, dma, dma, dma, dma((3,)),
         ],
         compiler_params=pltpu.CompilerParams(
@@ -574,9 +600,8 @@
     return pl.pallas_call(
         finish,
         out_shape=shapes,
-        in_specs=[anywhere] * 3,
-        out_specs=(anywhere,) * 3,
-        scratch_shapes=[dma((3,))],
+        in_specs=[vmem] * 3,
+        out_specs=(vmem,) * 3,
         compiler_params=pltpu.CompilerParams(vmem_limit_bytes=60 * 1024 * 1024),
     )(*grads)
 

time: 70.8 us -> 67.8 us (0.958)
  Pallas kernels: 70.1 us -> 67 us
    pallas_call x1, Pallas kernels: 6.34 us -> 1.59 us  [on_device(): pl.pallas_call(finish, out_shape=shapes, in_specs=[vmem] * 3, out_specs=(...]
    pallas_call x1, Pallas kernels: 63.7 us -> 65.4 us  [on_device(): pl.pallas_call(body, out_shape=shapes, in_specs=[anywhere] * 8, out_specs...]
where the time goes in v4:
time: 67.8 us; the launch traced here: 67.6 us
  Pallas kernels  67 us (99%)
    pallas_call x1, Pallas kernels, on_device(): pl.pallas_call(body, out_shape=shapes, in_specs=[anywhere] * 8, out_specs...  65.4 us
    pallas_call x1, Pallas kernels, on_device(): pl.pallas_call(finish, out_shape=shapes, in_specs=[vmem] * 3, out_specs=(...  1.59 us

profile of v4, /device:TPU:1, one launch (start us, length us, event | category | flops | bytes accessed | tf_op | source)
XLA Modules:
  0.0 67.6 jit_solution(10257902211087338570)
XLA Ops:
  0.6 65.4 %shard_map.103 = (bf16[256,256]{1,0:T(8,128)(2,1)}, f32[16,64]{1,0:T(8,128)}, f32[1,64,128]{2,1,0:T(8,128)}) custom-call(bf16[256,256]{1,0:T(8,128)(2,1)} %q_hbm.1, bf16[256,512]{1,0:T(8,128)(2,1)} %k_hbm.1, bf16[256,512]{1,0:T(8,128)(2,1)} %v_hbm.1, bf16[256,256]{1,0:T(8,128)(2,1)} %go_hbm.1, s32[2,128]{1,0:T(2,128)} %bitcast.3, s32[2]{0:T(128)} %bt_hbm.1, ...), custom_call_target="tpu_custom_call" | custom-call | flops 4000000000 | bytes 4000000 | tf_op jit(solution)/shard_map/pallas_call | solution.py:560
  66.0 1.6 %shard_map.104 = (bf16[256,256]{1,0:T(8,128)(2,1)}, f32[16,64]{1,0:T(8,128)}, f32[1,64,128]{2,1,0:T(8,128)}) custom-call(bf16[256,256]{1,0:T(8,128)(2,1)} %get-tuple-element.6.gq_in, f32[16,64]{1,0:T(8,128)} %get-tuple-element.7.glr_in, f32[1,64,128]{2,1,0:T(8,128)} %get-tuple-element.8.ga_in), custom_call_target="tpu_custom_call" | custom-call | tf_op jit(solution)/shard_map/pallas_call | solution.py:600

commit v5 on v4

--- a/solution.py
+++ b/solution.py
@@ -20,7 +20,10 @@
 EXP2_SCALE = HD ** (-0.5) * math.log2(math.e)
 FAR = -1e30
 MESH = pl.DeviceIdType.MESH
-ARRIVALS = (1, 7, 3, 5, 8 + 0, 8 + 3, 8 + 5, 2, 6, 4, 8 + 1, 8 + 7, 8 + 2, 8 + 6, 8 + 4)
+ARRIVALS = (1, 7, 2, 6, 8 + 0, 8 + 2, 8 + 6, 3, 5, 8 + 1, 8 + 7, 8 + 3, 8 + 5, 4, 8 + 4)
+ON_PLUS = sum(1 << code for code in (2, 8, 10, 11))
+ON_MINUS = sum(1 << code for code in (6, 5, 8, 14))
+Y_STEPS = (0, 2, -2,)
 EARLY = sum(code << (4 * i) for i, code in enumerate(ARRIVALS[:7]))
 LATE = sum(code << (4 * i) for i, code in enumerate(ARRIVALS[7:14]))
 LAST = ARRIVALS[14]
@@ -63,8 +66,8 @@
     sib = pair * 2 + (1 - core)
     z_plus = (y_hi * NZ + rem(z + 1, NZ)) * 2 + core
     z_minus = (y_hi * NZ + rem(z + NZ - 1, NZ)) * 2 + core
-    z_plus3 = (y_hi * NZ + rem(z + 3, NZ)) * 2 + core
-    z_minus3 = (y_hi * NZ + rem(z + NZ - 3, NZ)) * 2 + core
+    z_far_plus = (y_hi * NZ + rem(z + 2, NZ)) * 2 + core
+    z_far_minus = (y_hi * NZ + rem(z + NZ - 2, NZ)) * 2 + core
     x_plus = head * NX + rem(x + 1, NX)
     x_minus = head * NX + rem(x + NX - 1, NX)
 
@@ -81,13 +84,13 @@
 
     greet(z_plus, a)
     greet(z_minus, a)
-    greet(z_plus3, a)
-    greet(z_minus3, a)
+    greet(z_far_plus, a)
+    greet(z_far_minus, a)
     greet(sib, a)
 
     @pl.when(y_hi == 1)
     def _():
-        for step in (0, 3, -3):
+        for step in Y_STEPS:
             greet(y_ctx(step), y_adp)
 
     @pl.loop(1, N_ADP)
@@ -145,7 +148,7 @@
     own_k.wait()
     own_v.wait()
     x_k.wait()
-    pl.semaphore_wait(barrier, 5 + 3 * (1 - y_hi) + (N_ADP - 1) + N_CTX - selfdest)
+    pl.semaphore_wait(barrier, 5 + len(Y_STEPS) * (1 - y_hi) + (N_ADP - 1) + N_CTX - selfdest)
 
     def along(chunk, send_sem, to):
         ref = kv.at[chunk, mine]
@@ -171,14 +174,14 @@
     def to_y(which):
         return pltpu.make_async_remote_copy(
             src_ref=xkv, dst_ref=kv.at[c, mine], send_sem=y_send.at[which], recv_sem=mine_recv.at[c],
-            device_id={"ctx": y_ctx((0, 3, -3)[which]), "adp": y_adp}, device_id_type=MESH,
+            device_id={"ctx": y_ctx(Y_STEPS[which]), "adp": y_adp}, device_id_type=MESH,
         )
 
     def far(which):
         ref = kv.at[c, mine]
         return pltpu.make_async_remote_copy(
             src_ref=ref, dst_ref=ref, send_sem=far_send.at[which], recv_sem=mine_recv.at[c],
-            device_id={"ctx": (z_plus3, z_minus3)[which], "adp": a}, device_id_type=MESH,
+            device_id={"ctx": (z_far_plus, z_far_minus)[which], "adp": a}, device_id_type=MESH,
         )
 
     def await_mine(chunk):
@@ -201,7 +204,7 @@
 
     @pl.when(y_hi == 0)
     def _():
-        for which in range(3):
+        for which in range(len(Y_STEPS)):
             to_y(which).start()
 
     along(c, sib_send, sib).start()
@@ -348,8 +351,8 @@
         lower, off = div(code, 8), rem(code, 8)
         valid = (e >= 0) & (e < len(ARRIVALS)) & (lower <= y_hi)
         src_pair = (y_hi - lower) * NZ + rem(z + NZ - off, NZ)
-        on_plus = valid & ((off == 0) | (off == 5) | ((off == 3) & (lower == 1)))
-        on_minus = valid & ((off == 0) | (off == 3) | ((off == 5) & (lower == 0)))
+        on_plus = valid & ((lax.shift_right_logical(jnp.int32(ON_PLUS), code) & 1) == 1)
+        on_minus = valid & ((lax.shift_right_logical(jnp.int32(ON_MINUS), code) & 1) == 1)
         return valid, src_pair, on_plus, on_minus
 
     @pl.loop(0, len(ARRIVALS) + LAG_USE)
@@ -467,7 +470,7 @@
 
     @pl.when(y_hi == 0)
     def _():
-        for which in range(3):
+        for which in range(len(Y_STEPS)):
             to_y(which).wait_send()
 
     @pl.loop(0, len(ARRIVALS))
@@ -587,7 +590,7 @@
             pltpu.VMEM((N_ADP, 16, HD), F32),
             pltpu.VMEM((N_ADP, 16, HD), F32),
             dma((9,)), dma((N_CTX,)), dma((N_CTX,)), dma((N_CTX,)), dma((N_CTX,)),
-            dma((N_CTX,)), dma((N_CTX,)), dma((N_CTX,)), dma((3,)), dma((2,)),
+            dma((N_CTX,)), dma((N_CTX,)), dma((N_CTX,)), dma((len(Y_STEPS),)), dma((2,)),
             dma, dma, dma, dma, dma, dma, dma, dma, dma, dma, dma, dma, dma((3,)),
         ],
         compiler_params=pltpu.CompilerParams(

time: 67.8 us -> 65.4 us (0.965)
  Pallas kernels: 67 us -> 64.6 us
    pallas_call x1, Pallas kernels: 65.4 us -> 63 us  [on_device(): pl.pallas_call(body, out_shape=shapes, in_specs=[anywhere] * 8, out_specs...]
where the time goes in v5:
time: 65.4 us; the launch traced here: 65.3 us
  Pallas kernels  64.6 us (99%)
    pallas_call x1, Pallas kernels, on_device(): pl.pallas_call(body, out_shape=shapes, in_specs=[anywhere] * 8, out_specs...  63 us
    pallas_call x1, Pallas kernels, on_device(): pl.pallas_call(finish, out_shape=shapes, in_specs=[vmem] * 3, out_specs=(...  1.59 us

profile of v5, /device:TPU:1, one launch (start us, length us, event | category | flops | bytes accessed | tf_op | source)
XLA Modules:
  0.0 65.3 jit_solution(15869234959579529538)
XLA Ops:
  0.6 63.0 %shard_map.103 = (bf16[256,256]{1,0:T(8,128)(2,1)}, f32[16,64]{1,0:T(8,128)}, f32[1,64,128]{2,1,0:T(8,128)}) custom-call(bf16[256,256]{1,0:T(8,128)(2,1)} %q_hbm.1, bf16[256,512]{1,0:T(8,128)(2,1)} %k_hbm.1, bf16[256,512]{1,0:T(8,128)(2,1)} %v_hbm.1, bf16[256,256]{1,0:T(8,128)(2,1)} %go_hbm.1, s32[2,128]{1,0:T(2,128)} %bitcast.3, s32[2]{0:T(128)} %bt_hbm.1, ...), custom_call_target="tpu_custom_call" | custom-call | flops 4000000000 | bytes 4000000 | tf_op jit(solution)/shard_map/pallas_call | solution.py:563
  63.7 1.6 %shard_map.104 = (bf16[256,256]{1,0:T(8,128)(2,1)}, f32[16,64]{1,0:T(8,128)}, f32[1,64,128]{2,1,0:T(8,128)}) custom-call(bf16[256,256]{1,0:T(8,128)(2,1)} %get-tuple-element.6.gq_in, f32[16,64]{1,0:T(8,128)} %get-tuple-element.7.glr_in, f32[1,64,128]{2,1,0:T(8,128)} %get-tuple-element.8.ga_in), custom_call_target="tpu_custom_call" | custom-call | tf_op jit(solution)/shard_map/pallas_call | solution.py:603

commit v6 on v5

--- a/solution.py
+++ b/solution.py
@@ -27,7 +27,7 @@
 EARLY = sum(code << (4 * i) for i, code in enumerate(ARRIVALS[:7]))
 LATE = sum(code << (4 * i) for i, code in enumerate(ARRIVALS[7:14]))
 LAST = ARRIVALS[14]
-LAG_SWAP, LAG_USE = 3, 5
+LAG_SWAP, LAG_USE = 2, 4
 F32 = jnp.float32
 BF16 = jnp.bfloat16
 
@@ -376,6 +376,17 @@
             swap(chunk, HALF, x_minus).start()
             along(chunk, sib_send, sib).start()
 
+        whole, last_pair, _, _ = event(e - LAG_USE)
+
+        @pl.when(whole)
+        def _():
+            await_mine(last_pair * 2 + 1 - core)
+            await_other(last_pair * 2 + 1 - core)
+
+        @pl.when(whole & (last_pair < pair))
+        def _():
+            attend(last_pair, False)
+
         ready, src_pair, _, _ = event(e - LAG_SWAP)
         chunk2 = src_pair * 2 + core
 
@@ -383,17 +394,6 @@
         def _():
             await_other(chunk2)
             rest_to_sib(chunk2).start()
-
-        whole, last_pair, _, _ = event(e - LAG_USE)
-
-        @pl.when(whole)
-        def _():
-            await_mine(last_pair * 2 + 1 - core)
-            await_other(last_pair * 2 + 1 - core)
-
-        @pl.when(whole & (last_pair < pair))
-        def _():
-            attend(last_pair, False)
 
     b_all(b_recv).wait()
     own_b.wait()

time: 65.4 us -> 64.7 us (0.989)
  Pallas kernels: 64.6 us -> 63.9 us
    pallas_call x1, Pallas kernels: 63 us -> 62.3 us  [on_device(): pl.pallas_call(body, out_shape=shapes, in_specs=[anywhere] * 8, out_specs...]
where the time goes in v6:
time: 64.7 us; the launch traced here: 64.6 us
  Pallas kernels  63.9 us (99%)
    pallas_call x1, Pallas kernels, on_device(): pl.pallas_call(body, out_shape=shapes, in_specs=[anywhere] * 8, out_specs...  62.3 us
    pallas_call x1, Pallas kernels, on_device(): pl.pallas_call(finish, out_shape=shapes, in_specs=[vmem] * 3, out_specs=(...  1.59 us

profile of v6, /device:TPU:1, one launch (start us, length us, event | category | flops | bytes accessed | tf_op | source)
XLA Modules:
  0.0 64.6 jit_solution(1620514471089449580)
XLA Ops:
  0.6 62.3 %shard_map.103 = (bf16[256,256]{1,0:T(8,128)(2,1)}, f32[16,64]{1,0:T(8,128)}, f32[1,64,128]{2,1,0:T(8,128)}) custom-call(bf16[256,256]{1,0:T(8,128)(2,1)} %q_hbm.1, bf16[256,512]{1,0:T(8,128)(2,1)} %k_hbm.1, bf16[256,512]{1,0:T(8,128)(2,1)} %v_hbm.1, bf16[256,256]{1,0:T(8,128)(2,1)} %go_hbm.1, s32[2,128]{1,0:T(2,128)} %bitcast.3, s32[2]{0:T(128)} %bt_hbm.1, ...), custom_call_target="tpu_custom_call" | custom-call | flops 4000000000 | bytes 4000000 | tf_op jit(solution)/shard_map/pallas_call | solution.py:563
  63.0 1.6 %shard_map.104 = (bf16[256,256]{1,0:T(8,128)(2,1)}, f32[16,64]{1,0:T(8,128)}, f32[1,64,128]{2,1,0:T(8,128)}) custom-call(bf16[256,256]{1,0:T(8,128)(2,1)} %get-tuple-element.6.gq_in, f32[16,64]{1,0:T(8,128)} %get-tuple-element.7.glr_in, f32[1,64,128]{2,1,0:T(8,128)} %get-tuple-element.8.ga_in), custom_call_target="tpu_custom_call" | custom-call | tf_op jit(solution)/shard_map/pallas_call | solution.py:603

commit v7 on v6

--- a/solution.py
+++ b/solution.py
@@ -20,10 +20,10 @@
 EXP2_SCALE = HD ** (-0.5) * math.log2(math.e)
 FAR = -1e30
 MESH = pl.DeviceIdType.MESH
-ARRIVALS = (1, 7, 2, 6, 8 + 0, 8 + 2, 8 + 6, 3, 5, 8 + 1, 8 + 7, 8 + 3, 8 + 5, 4, 8 + 4)
-ON_PLUS = sum(1 << code for code in (2, 8, 10, 11))
-ON_MINUS = sum(1 << code for code in (6, 5, 8, 14))
-Y_STEPS = (0, 2, -2,)
+ARRIVALS = (1, 7, 8 + 0, 2, 6, 8 + 1, 8 + 7, 3, 5, 8 + 2, 8 + 6, 4, 8 + 3, 8 + 5, 8 + 4)
+ON_PLUS = sum(1 << code for code in (1, 2, 8, 9, 10, 11))
+ON_MINUS = sum(1 << code for code in (7, 6, 5, 8, 15, 14))
+Y_STEPS = (0,)
 EARLY = sum(code << (4 * i) for i, code in enumerate(ARRIVALS[:7]))
 LATE = sum(code << (4 * i) for i, code in enumerate(ARRIVALS[7:14]))
 LAST = ARRIVALS[14]
@@ -49,7 +49,7 @@
     gq_hbm, glr_hbm, ga_hbm,
     kv, xkv, q_ref, go_ref, docs_ref, bt_ref, low_ref, gq_ref, glr_ref, ga_ref,
     acc, row_top, qdoc, bcols, bt_mine, btile, lowt, pbuf, qbuf, tbuf, gbuf, rsend, rbuf,
-    loc_sem, mine_recv, other_recv, plus_send, minus_send, sib_send, sib2_send, x_send, y_send, far_send,
+    loc_sem, mine_recv, other_recv, plus_send, minus_send, sib_send, sib2_send, x_send, y_send,
     bt_recv, bt_send, b_recv, b_send, bs_recv, bs_send,
     r_recv, r_send, p_recv, p_send, g_recv, g_send, out_sem,
 ):
@@ -66,8 +66,6 @@
     sib = pair * 2 + (1 - core)
     z_plus = (y_hi * NZ + rem(z + 1, NZ)) * 2 + core
     z_minus = (y_hi * NZ + rem(z + NZ - 1, NZ)) * 2 + core
-    z_far_plus = (y_hi * NZ + rem(z + 2, NZ)) * 2 + core
-    z_far_minus = (y_hi * NZ + rem(z + NZ - 2, NZ)) * 2 + core
     x_plus = head * NX + rem(x + 1, NX)
     x_minus = head * NX + rem(x + NX - 1, NX)
 
@@ -84,8 +82,6 @@
 
     greet(z_plus, a)
     greet(z_minus, a)
-    greet(z_far_plus, a)
-    greet(z_far_minus, a)
     greet(sib, a)
 
     @pl.when(y_hi == 1)
@@ -148,7 +144,7 @@
     own_k.wait()
     own_v.wait()
     x_k.wait()
-    pl.semaphore_wait(barrier, 5 + len(Y_STEPS) * (1 - y_hi) + (N_ADP - 1) + N_CTX - selfdest)
+    pl.semaphore_wait(barrier, 3 + len(Y_STEPS) * (1 - y_hi) + (N_ADP - 1) + N_CTX - selfdest)
 
     def along(chunk, send_sem, to):
         ref = kv.at[chunk, mine]
@@ -175,13 +171,6 @@
         return pltpu.make_async_remote_copy(
             src_ref=xkv, dst_ref=kv.at[c, mine], send_sem=y_send.at[which], recv_sem=mine_recv.at[c],
             device_id={"ctx": y_ctx(Y_STEPS[which]), "adp": y_adp}, device_id_type=MESH,
-        )
-
-    def far(which):
-        ref = kv.at[c, mine]
-        return pltpu.make_async_remote_copy(
-            src_ref=ref, dst_ref=ref, send_sem=far_send.at[which], recv_sem=mine_recv.at[c],
-            device_id={"ctx": (z_far_plus, z_far_minus)[which], "adp": a}, device_id_type=MESH,
         )
 
     def await_mine(chunk):
@@ -199,8 +188,6 @@
     along(c, plus_send, z_plus).start()
     along(c, minus_send, z_minus).start()
 
-    far(0).start()
-    far(1).start()
 
     @pl.when(y_hi == 0)
     def _():
@@ -465,8 +452,6 @@
     along(c, sib_send, sib).wait_send()
     rest_to_sib(c).wait_send()
 
-    far(0).wait_send()
-    far(1).wait_send()
 
     @pl.when(y_hi == 0)
     def _():
@@ -590,7 +575,7 @@
             pltpu.VMEM((N_ADP, 16, HD), F32),
             pltpu.VMEM((N_ADP, 16, HD), F32),
             dma((9,)), dma((N_CTX,)), dma((N_CTX,)), dma((N_CTX,)), dma((N_CTX,)),
-            dma((N_CTX,)), dma((N_CTX,)), dma((N_CTX,)), dma((len(Y_STEPS),)), dma((2,)),
+            dma((N_CTX,)), dma((N_CTX,)), dma((N_CTX,)), dma((len(Y_STEPS),)),
             dma, dma, dma, dma, dma, dma, dma, dma, dma, dma, dma, dma, dma((3,)),
         ],
         compiler_params=pltpu.CompilerParams(

time: 64.7 us -> 64.1 us (level)
  no operation moved by 1% of the time
where the time goes in v7:
time: 64.1 us; the launch traced here: 63.9 us
  Pallas kernels  63.3 us (99%)
    pallas_call x1, Pallas kernels, on_device(): pl.pallas_call(body, out_shape=shapes, in_specs=[anywhere] * 8, out_specs...  61.7 us
    pallas_call x1, Pallas kernels, on_device(): pl.pallas_call(finish, out_shape=shapes, in_specs=[vmem] * 3, out_specs=(...  1.59 us

profile of v7, /device:TPU:1, one launch (start us, length us, event | category | flops | bytes accessed | tf_op | source)
XLA Modules:
  0.0 63.9 jit_solution(4465174676775831429)
XLA Ops:
  0.6 61.7 %shard_map.103 = (bf16[256,256]{1,0:T(8,128)(2,1)}, f32[16,64]{1,0:T(8,128)}, f32[1,64,128]{2,1,0:T(8,128)}) custom-call(bf16[256,256]{1,0:T(8,128)(2,1)} %q_hbm.1, bf16[256,512]{1,0:T(8,128)(2,1)} %k_hbm.1, bf16[256,512]{1,0:T(8,128)(2,1)} %v_hbm.1, bf16[256,256]{1,0:T(8,128)(2,1)} %go_hbm.1, s32[2,128]{1,0:T(2,128)} %bitcast.3, s32[2]{0:T(128)} %bt_hbm.1, ...), custom_call_target="tpu_custom_call" | custom-call | flops 4000000000 | bytes 4000000 | tf_op jit(solution)/shard_map/pallas_call | solution.py:548
  62.3 1.6 %shard_map.104 = (bf16[256,256]{1,0:T(8,128)(2,1)}, f32[16,64]{1,0:T(8,128)}, f32[1,64,128]{2,1,0:T(8,128)}) custom-call(bf16[256,256]{1,0:T(8,128)(2,1)} %get-tuple-element.6.gq_in, f32[16,64]{1,0:T(8,128)} %get-tuple-element.7.glr_in, f32[1,64,128]{2,1,0:T(8,128)} %get-tuple-element.8.ga_in), custom_call_target="tpu_custom_call" | custom-call | tf_op jit(solution)/shard_map/pallas_call | solution.py:588
